TPU v7x, 256 devices: a whole 4x4x8 slice. The times are simulated.
256 devices in a mesh: sens: 64 (over y, z_hi, x, core), beam: 4 (over z_lo).
Axes of the slice: x: 4, y: 4, z: 8 (z_hi: 2, z_lo: 4; z = z_hi * 4 + z_lo), core: 2. Of those that a mesh axis runs over, the one named last changes fastest.
Arguments:
- samples: bfloat16 [16384, 64, 1024], P('sens', 'beam'), may hold values from -6 to 6
- weights: bfloat16 [2, 32, 16384, 512], P(None, None, 'sens', 'beam'), may hold values from -0.046875 to 0.046875
- chosen_frequency_bins: int32 [32], replicated, may hold values from 1 to 511
Outputs:
- cross_spectra: float32 [2, 64, 512, 256], P(None, 'sens', 'beam')
Inputs may be any that keep to these rules, and one draw needn't show every extreme that they name: `chosen_frequency_bins`: channel bins, possibly repeated.
All inputs are finite; a program needn't handle non-finite values.
Results may differ from a plain program's by a relative error of at most 0.0051.
Values may be sent and summed in bfloat16 or wider, within the bound.
No kernel may reach another device: no remote copies, remote signals or barrier semaphores. Data moves between devices by JAX's collectives and lax.ppermute only.
A program may use at most 128 MiB of HBM per device.

v0:
```python
import math

import jax
import jax.numpy as jnp
from jax import lax
from jax.sharding import PartitionSpec as P


def from_partner(x, axis, bit):
    return lax.ppermute(x, axis, [(i, i ^ 1 << bit) for i in range(lax.axis_size(axis))])


def dft_table(chosen_frequency_bins, fourier_length):
    clock_ticks = jnp.arange(fourier_length, dtype=jnp.int32)
    rotation_radians = clock_ticks[:, None] * chosen_frequency_bins[None, :] % fourier_length
    angles = 2.0 * math.pi / fourier_length * rotation_radians.astype(jnp.float32)
    hann_envelope = 0.5 - 0.5 * jnp.cos(
        2.0 * math.pi / fourier_length * clock_ticks.astype(jnp.float32)
    )
    scaling = (hann_envelope / math.sqrt(fourier_length))[:, None]
    return jnp.concatenate([scaling * jnp.cos(angles), -scaling * jnp.sin(angles)], axis=1).astype(
        jnp.bfloat16
    )


def contract(left, right):
    return lax.dot_general(
        left,
        right,
        (((0,), (0,)), ((), ())),
        precision=lax.Precision.HIGHEST,
        preferred_element_type=jnp.float32,
    )


def gram_block(left, piece, inverse):
    real_g = contract(left[:, 0], piece[:, 0]) + contract(left[:, 1], piece[:, 1])
    imag_g = contract(left[:, 1], piece[:, 0]) - contract(left[:, 0], piece[:, 1])
    return jnp.stack([real_g * inverse, imag_g * inverse])


def steered_array_responses(real_x, imag_x, weight_real, imag_w, form):
    output_real = jnp.einsum(
        form, real_x, weight_real, preferred_element_type=jnp.float32
    ) - jnp.einsum(form, imag_x, imag_w, preferred_element_type=jnp.float32)
    imag_y = jnp.einsum(form, real_x, imag_w, preferred_element_type=jnp.float32) + jnp.einsum(
        form, imag_x, weight_real, preferred_element_type=jnp.float32
    )
    return jnp.concatenate([output_real, imag_y], axis=-1)


def local(samples, weights, chosen_frequency_bins):
    sens_local, snap_local, fourier_length = samples.shape
    chans = chosen_frequency_bins.shape[0]
    beams_local = weights.shape[3]
    table = dft_table(chosen_frequency_bins, fourier_length)
    spectra = jnp.dot(
        samples.reshape(sens_local * snap_local, fourier_length),
        table,
        preferred_element_type=jnp.float32,
    ).astype(jnp.bfloat16)
    spectra = (
        spectra.reshape(sens_local, snap_local, 2, chans)
        .transpose(3, 1, 2, 0)
        .reshape(chans, snap_local, 2 * sens_local)
    )
    gathered = lax.all_gather(spectra, "beam", axis=1, tiled=True)
    snapshots = gathered.shape[1]
    half_snaps = snapshots // 2
    rows_total = chans * 2
    covered = min(chans, rows_total // lax.axis_size("sens") * lax.axis_size("sens") // 2 + 1)
    real_x = gathered[:, :, :sens_local]
    imag_x = gathered[:, :, sens_local:]
    weight_real = weights[0]
    imag_w = weights[1]
    term = steered_array_responses(real_x, imag_x, weight_real, imag_w, "cns,csb->cnb")
    term = term.reshape(covered * 2, half_snaps, 2 * beams_local)
    beamed = lax.psum_scatter(term, "sens", scatter_dimension=0, tiled=True)
    owned_beams = beamed[0].reshape(half_snaps, 2, beams_local)
    inverse = 1.0 / snapshots
    parity = lax.axis_index("sens") % 2
    beam_count = beams_local * lax.axis_size("beam")
    midway_column_span = beam_count // 2
    partial_value = gram_block(
        owned_beams, lax.all_gather(owned_beams, "beam", axis=2, tiled=True), inverse
    )
    outgoing = lax.dynamic_slice_in_dim(
        partial_value, (1 - parity) * midway_column_span, midway_column_span, 2
    )
    returned = from_partner(outgoing, "sens", 0)
    kept = (
        lax.dynamic_slice_in_dim(partial_value, parity * midway_column_span, midway_column_span, 2)
        + returned
    )
    return kept.reshape(2, 1, beams_local, midway_column_span)


def solution(mesh):
    return jax.shard_map(
        local,
        mesh=mesh,
        in_specs=(P("sens", "beam", None), P(None, None, "sens", "beam"), P()),
        out_specs=P(None, "sens", "beam", None),
        check_vma=False,
    )
```

profile of v0, /device:TPU:1, one launch (start us, length us, event | category | flops | bytes accessed | tf_op | source)
XLA Modules:
  0.0 516.8 jit_solution(1277946655387020212)
XLA Ops:
  6.5 0.0 all-gather.2.cloned.1.call-start
  6.6 1.3 multiply_convert_fusion.1
  7.8 6.0 %fusion = bf16[4096,64]{0,1:T(8,128)(2,1)S(1)} fusion(bf16[4096,1024]{1,0:T(8,128)(2,1)} %bitcast.45, bf16[1024,32]{0,1:T(8,128)(2,1)S(1)} %get-tuple-element.10, bf16[1024,32]{0,1:T(8,128)(2,1)S(1)} %get-tuple-element.9), kind=kOutput, calls=%fused_computation.1 | convolution fusion | flops 537395200 | bytes 9043968 | tf_op jit(solution)/shard_map/dot_general | solution.py:57
  13.9 0.5 copy.9
  14.4 0.8 reshape.30
  15.2 2.1 copy.10
  17.3 1.1 reshape.31
  18.4 0.0 all-gather.2.cloned.1.call-update
  18.5 0.0 reduce-scatter.2.cloned.1.call-start
  18.5 54.0 %all-gather.2.cloned.1.call-done = bf16[32,64,512]{2,1,0:T(8,128)(2,1)} async-done(((bf16[32,16,512]{2,1,0:T(8,128)(2,1)}), bf16[32,64,512]{2,1,0:T(8,128)(2,1)}) %all-gather.2.cloned.1.call-update) | async-done | bytes 2097168 | tf_op jit(solution)/shard_map/all_gather | solution.py:67
  72.5 0.0 copy-start
  72.5 2.6 fusion.3
  75.0 0.6 copy-done
  75.6 0.0 copy-start.1
  75.6 1.9 fusion.1
  77.5 0.0 copy-done.1
  77.5 0.5 fusion.13
  78.1 0.5 fusion.16
  78.6 1.5 pad_maximum_fusion
  80.1 0.0 reduce-scatter.2.cloned.1.call-update
  80.2 405.3 %reduce-scatter.2.cloned.1.call-done = f32[1,32,256]{2,1,0:T(8,128)} async-done(((f32[64,32,256]{2,1,0:T(8,128)}), f32[1,32,256]{2,1,0:T(8,128)}) %reduce-scatter.2.cloned.1.call-update) | async-done | bytes 32784 | tf_op jit(solution)/shard_map/reduce_scatter | solution.py:78
  485.5 0.8 reshape_squeeze.3
  486.2 10.2 %all_gather.7 = f32[32,2,512]{2,1,0:T(2,128)S(1)} all-gather(f32[32,2,128]{2,1,0:T(2,128)S(1)} %reshape_squeeze.3), channel_id=1, replica_groups=mesh['sens'=64,'beam'=4] {'beam'}, dimensions={2}, use_global_device_ids=true | all-gather | bytes 163840 | tf_op jit(solution)/shard_map/all_gather | solution.py:85
  496.5 0.1 fusion.52
  496.6 0.4 fusion.42
  497.0 0.4 fusion.44
  497.4 0.4 fusion.20
  497.9 0.4 fusion.22
  498.3 9.7 %collective-permute-start = (f32[2,128,256]{2,1,0:T(8,128)S(1)}, f32[2,128,256]{2,1,0:T(8,128)S(1)}, u32[]{:S(2)}, u32[]{:S(2)}) collective-permute-start(f32[2,128,256]{2,1,0:T(8,128)S(1)} %fusion.27), channel_id=1, source_target_pairs={{0,4},{4,0},{8,12},{12,8},{16,20},{20,16},{24,28},{28,24},{32,36},... | collective-permute-start | bytes 786440 | tf_op jit(solution)/shard_map/ppermute | solution.py:10
  508.0 1.2 collective-permute-done
  509.2 0.7 fusion.30
  (3 shorter events, 0.1 us)
Async XLA Ops:
  6.5 65.9 %all-gather.2.cloned.1.call-start = ((), (), s32[]{:S(2)}) async-start(), calls=%async_computation.1 | async-start | bytes 2621440 | tf_op jit(solution)/shard_map/all_gather | solution.py:67
  18.5 467.0 %reduce-scatter.2.cloned.1.call-start = ((), (), s32[]{:S(2)}) async-start(), calls=%async_computation.2 | async-start | bytes 2129920 | tf_op jit(solution)/shard_map/reduce_scatter | solution.py:78
  72.5 3.1 copy-start
  75.6 1.9 copy-start.1
  498.3 10.8 %collective-permute-start = (f32[2,128,256]{2,1,0:T(8,128)S(1)}, f32[2,128,256]{2,1,0:T(8,128)S(1)}, u32[]{:S(2)}, u32[]{:S(2)}) collective-permute-start(f32[2,128,256]{2,1,0:T(8,128)S(1)} %fusion.27), channel_id=1, source_target_pairs={{0,4},{4,0},{8,12},{12,8},{16,20},{20,16},{24,28},{28,24},{32,36},... | collective-permute-start | bytes 786440 | tf_op jit(solution)/shard_map/ppermute | solution.py:10
Sparse Core Ops, SparseCore 0:
  18.6 53.8 all-gather.1
  80.3 405.1 reduce-scatter.1
where the time goes:
time: 517 us
  waiting for transfers between devices  460 us (89%)
  between operations  13.5 us (3%)
  matrix products  13.2 us (3%)
  blocking collectives  10.2 us (2%)
  starting transfers between devices  9.71 us (2%)
  local copies, waits for them, and re-layouts  6.04 us (1%)
    reduce_scatter x1, waiting for transfers between devices, local(): beamed = lax.psum_scatter(term, 'sens', scatter_dimension=0, tiled=True)  405 us
    all_gather x1, waiting for transfers between devices, local(): gathered = lax.all_gather(spectra, 'beam', axis=1, tiled=True)  54 us
  transfers between devices with their start and end apart: 3, of which 3 were waited for; matrix products, arithmetic and copies ran while one was open for 0% of the time, Pallas kernels for 0%

commit v1 on v0

v1 whole, which is shorter than its diff:
```python
import math

import jax
import jax.numpy as jnp
from jax import lax
from jax.sharding import Mesh, PartitionSpec as P

AXES = ("y", "zh", "x", "core", "q")
NEAR = [(0, 1), (1, 0), (2, 3), (3, 2)]
MIDDLE = [(1, 2), (2, 1)]
FAR = [(0, 2), (2, 0), (1, 3), (3, 1)]
FORWARD = [(2, 3), (1, 0)]
SWAP = [(0, 1), (1, 0)]


def dft_table(chosen_frequency_bins, fourier_length):
    clock_ticks = jnp.arange(fourier_length, dtype=jnp.int32)
    rotation_radians = clock_ticks[:, None] * chosen_frequency_bins[None, :] % fourier_length
    angles = 2.0 * math.pi / fourier_length * rotation_radians.astype(jnp.float32)
    hann_envelope = 0.5 - 0.5 * jnp.cos(
        2.0 * math.pi / fourier_length * clock_ticks.astype(jnp.float32)
    )
    scaling = (hann_envelope / math.sqrt(fourier_length))[:, None]
    return jnp.concatenate([scaling * jnp.cos(angles), -scaling * jnp.sin(angles)], axis=1).astype(
        jnp.bfloat16
    )


def contract(left, right):
    return lax.dot_general(
        left,
        right,
        (((0,), (0,)), ((), ())),
        precision=lax.Precision.HIGHEST,
        preferred_element_type=jnp.float32,
    )


def local(samples, weights, chosen_frequency_bins):
    sens_local, snap_local, fourier_length = samples.shape
    chans = chosen_frequency_bins.shape[0]
    beams_local = weights.shape[3]
    core = lax.axis_index("core")
    q = lax.axis_index("q")
    table = dft_table(chosen_frequency_bins, fourier_length)
    spectra = jnp.dot(
        samples.reshape(sens_local * snap_local, fourier_length),
        table,
        preferred_element_type=jnp.float32,
    ).astype(jnp.bfloat16)
    spectra = spectra.reshape(sens_local, snap_local, 2, chans).transpose(2, 3, 1, 0)
    far = lax.ppermute(spectra, "q", FAR)
    near = lax.ppermute(spectra, "q", NEAR)
    middle = lax.ppermute(spectra, "q", MIDDLE)
    forward = lax.ppermute(far, "q", FORWARD)
    third = jnp.where((q == 1) | (q == 2), middle, forward)
    every = jnp.concatenate([spectra, near, far, third], axis=2)
    real_x, imag_x = every[0], every[1]
    form = "cns,csb->cnb"
    dot = lambda a, b: jnp.einsum(form, a, b, preferred_element_type=jnp.float32)
    real_y = dot(real_x, weights[0]) - dot(imag_x, weights[1])
    imag_y = dot(real_x, weights[1]) + dot(imag_x, weights[0])
    mine = jnp.where(core == 0, real_y, imag_y)
    other = jnp.where(core == 0, imag_y, real_y)
    snaps = mine.shape[1]
    mine = mine + lax.ppermute(other.astype(jnp.bfloat16), "core", SWAP).astype(jnp.float32)
    mine = (
        mine.reshape(4, 2, 4, snaps, beams_local)
        .transpose(0, 2, 1, 3, 4)
        .astype(jnp.bfloat16)
        .reshape(16, 2, snaps, beams_local)
    )
    mine = lax.all_to_all(mine, ("y", "x"), 0, 0)
    mine = jnp.sum(mine.astype(jnp.float32), axis=0)
    mine = jnp.broadcast_to(mine[:, None], (2, 4, snaps, beams_local)).reshape(
        8, snaps, beams_local
    )
    mine = lax.all_to_all(mine, ("zh", "q"), 0, 0).reshape(2, 4, snaps, beams_local)
    mine = mine[0] + mine[1]
    mine = mine.reshape(4, 4, snaps // 4, beams_local)
    mine = jnp.stack(
        [mine[b, jnp.array([k ^ b for k in range(4)])] for b in range(4)]
    ).reshape(4, snaps, beams_local)
    other = lax.ppermute(mine, "core", SWAP)
    real_y = jnp.where(core == 0, mine, other)
    imag_y = jnp.where(core == 0, other, mine)
    inverse = 1.0 / snaps
    rows = lambda a: lax.dynamic_index_in_dim(a, q, 0, keepdims=False)
    columns = lambda a: (
        lax.dynamic_slice_in_dim(a, 2 * core, 2, 0)
        .transpose(1, 0, 2)
        .reshape(snaps, 2 * beams_local)
    )
    left_real, left_imag = rows(real_y), rows(imag_y)
    right = jnp.concatenate([columns(real_y), columns(imag_y)], axis=0)
    real_g = contract(jnp.concatenate([left_real, left_imag], axis=0), right)
    imag_g = contract(jnp.concatenate([left_imag, -left_real], axis=0), right)
    return jnp.stack([real_g * inverse, imag_g * inverse])[:, None]


def solution(mesh):
    fine = Mesh(mesh.devices.reshape(4, 2, 4, 2, 4), AXES)
    sens = ("y", "zh", "x", "core")
    return jax.shard_map(
        local,
        mesh=fine,
        in_specs=(P(sens, "q", None), P(None, None, sens, "q"), P()),
        out_specs=P(None, sens, "q", None),
        check_vma=False,
    )
```

time: 517 us -> 114 us (0.22)
  waiting for transfers between devices: 460 us -> 52.7 us
  starting transfers between devices: 9.71 us -> 24.1 us
  between operations: 13.5 us -> 0.28 us
  blocking collectives: 10.2 us -> 18 us
    reduce_scatter x1 -> x0, waiting for transfers between devices: 405 us -> none  [local(): beamed = lax.psum_scatter(term, 'sens', scatter_dimension=0, tiled=True)]
    all_gather x1 -> x0, waiting for transfers between devices: 54 us -> none  [local(): gathered = lax.all_gather(spectra, 'beam', axis=1, tiled=True)]
    ppermute x1 -> x6, waiting for transfers between devices: 1.16 us -> 43.6 us  [the longest x1 21.5 us: local(): far = lax.ppermute(spectra, 'q', FAR)]
    all_to_all x0 -> x1, blocking collectives: none -> 18 us  [local(): mine = lax.all_to_all(mine, ('y', 'x'), 0, 0)]
    all_gather x1 -> x0, blocking collectives: 10.2 us -> none  [local(): lax.all_gather(owned_beams, 'beam', axis=2, tiled=True)]
    all_to_all x0 -> x1, waiting for transfers between devices: none -> 9.19 us  [local(): lax.all_to_all(mine, ('zh', 'q'), 0, 0).reshape(2, 4, snaps, beams_local)]
    all_to_all x0 -> x1, starting transfers between devices: none -> 7.8 us  [local(): lax.all_to_all(mine, ('zh', 'q'), 0, 0).reshape(2, 4, snaps, beams_local)]
    ppermute x1 -> x6, starting transfers between devices: 9.67 us -> 16.3 us  [the longest x1 4.45 us: local(): lax.ppermute(other.astype(jnp.bfloat16), 'core', SWAP).astype(jnp.float32)]
  transfers between devices with their start and end apart: 3 -> 7, of which waited for: 3 -> 6; matrix products, arithmetic and copies ran while one was open for 0% -> 0% of each run, Pallas kernels for 0% -> 0%
where the time goes in v1:
time: 114 us; the launch traced here: 113 us
  waiting for transfers between devices  52.7 us (46%)
  starting transfers between devices  24.1 us (21%)
  blocking collectives  18 us (16%)
  matrix products  8.79 us (8%)
  local copies, waits for them, and re-layouts  6.5 us (6%)
  other arithmetic  3.02 us (3%)
    ppermute x1, waiting for transfers between devices, local(): far = lax.ppermute(spectra, 'q', FAR)  21.5 us
    all_to_all x1, blocking collectives, local(): mine = lax.all_to_all(mine, ('y', 'x'), 0, 0)  18 us
    ppermute x1, waiting for transfers between devices, local(): near = lax.ppermute(spectra, 'q', NEAR)  11.2 us
    all_to_all x1, waiting for transfers between devices, local(): lax.all_to_all(mine, ('zh', 'q'), 0, 0).reshape(2, 4, snaps, beams_local)  9.19 us
    ppermute x1, waiting for transfers between devices, local(): forward = lax.ppermute(far, 'q', FORWARD)  8.37 us
    all_to_all x1, starting transfers between devices, local(): lax.all_to_all(mine, ('zh', 'q'), 0, 0).reshape(2, 4, snaps, beams_local)  7.8 us
    dot_general x1, matrix products, local(): jnp.dot(samples.reshape(sens_local * snap_local, fourier_length), table,...  6.04 us
    ppermute x1, starting transfers between devices, local(): lax.ppermute(other.astype(jnp.bfloat16), 'core', SWAP).astype(jnp.float32)  4.45 us
  transfers between devices with their start and end apart: 7, of which 6 were waited for; matrix products, arithmetic and copies ran while one was open for 0% of the time, Pallas kernels for 0%

profile of v1, /device:TPU:1, one launch (start us, length us, event | category | flops | bytes accessed | tf_op | source)
XLA Modules:
  0.0 113.4 jit_solution(16638647615922162374)
XLA Ops:
  0.0 1.3 %multiply_convert_fusion.1 = (bf16[1024,32]{0,1:T(8,128)(2,1)S(1)}, bf16[1024,32]{0,1:T(8,128)(2,1)S(1)}) fusion(s32[32]{0:T(128)} %param.9, f32[1024]{0:T(1024)S(1)} %get-tuple-element.11, f32[1024]{0:T(1024)S(1)} %get-tuple-element.12), kind=kLoop, calls=%fused_computation.44 | loop fusion | flops 589824 | bytes 139392 | tf_op jit(solution)/shard_map/convert
  1.3 6.0 %fusion = bf16[4096,64]{0,1:T(8,128)(2,1)S(1)} fusion(bf16[4096,1024]{1,0:T(8,128)(2,1)} %bitcast.61, bf16[1024,32]{0,1:T(8,128)(2,1)S(1)} %get-tuple-element.8, bf16[1024,32]{0,1:T(8,128)(2,1)S(1)} %get-tuple-element.7), kind=kOutput, calls=%fused_computation.5 | convolution fusion | flops 537395200 | bytes 9043968 | tf_op jit(solution)/shard_map/dot_general | solution.py:46
  7.4 0.5 copy.14
  7.8 0.8 reshape.54
  8.7 2.0 %copy.15 = bf16[256,16,2,32]{0,1,3,2:T(8,128)(2,1)S(1)} copy(bf16[256,16,2,32]{3,2,1,0:T(2,128)(2,1)S(1)} %reshape.54) | data formatting | bytes 1048576 | tf_op jit(solution)/shard_map/reshape | solution.py:51
  10.7 3.9 %collective-permute-start.1 = (bf16[2,32,16,256]{3,2,1,0:T(8,128)(2,1)S(1)}, bf16[2,32,16,256]{3,2,1,0:T(8,128)(2,1)S(1)}, u32[]{:S(2)}, u32[]{:S(2)}) collective-permute-start(bf16[2,32,16,256]{3,2,1,0:T(8,128)(2,1)S(1)} %bitcast.64), channel_id=1, source_target_pairs={{0,2},{2,0},{1,3},{3,1},{4,6},{6,4},{5,7},{7,5},{8,10},{10,8},{9,1... | collective-permute-start | bytes 1572872 | tf_op jit(solution)/shard_map/ppermute | solution.py:52
  14.6 0.7 collective-permute-start.2
  15.3 21.5 %collective-permute-done.1 = bf16[2,32,16,256]{3,2,1,0:T(8,128)(2,1)S(1)} collective-permute-done((bf16[2,32,16,256]{3,2,1,0:T(8,128)(2,1)S(1)}, bf16[2,32,16,256]{3,2,1,0:T(8,128)(2,1)S(1)}, u32[]{:S(2)}, u32[]{:S(2)}) %collective-permute-start.1) | collective-permute-done | bytes 524320 | tf_op jit(solution)/shard_map/ppermute | solution.py:52
  36.8 1.3 %collective-permute-start.3 = (bf16[2,32,16,256]{3,2,1,0:T(8,128)(2,1)S(1)}, bf16[2,32,16,256]{3,2,1,0:T(8,128)(2,1)S(1)}, u32[]{:S(2)}, u32[]{:S(2)}) collective-permute-start(bf16[2,32,16,256]{3,2,1,0:T(8,128)(2,1)S(1)} %collective-permute-done.1), channel_id=1, source_target_pairs={{2,3},{1,0},{6,7},{5,4},{10,11},{9,8},{14,15},{13,12},{18,19},{17,... | collective-permute-start | bytes 1572872 | tf_op jit(solution)/shard_map/ppermute | solution.py:55
  38.1 2.2 %collective-permute-start = (bf16[2,32,16,256]{3,2,1,0:T(8,128)(2,1)S(1)}, bf16[2,32,16,256]{3,2,1,0:T(8,128)(2,1)S(1)}, u32[]{:S(2)}, u32[]{:S(2)}) collective-permute-start(bf16[2,32,16,256]{3,2,1,0:T(8,128)(2,1)S(1)} %bitcast.66), channel_id=1, source_target_pairs={{0,1},{1,0},{2,3},{3,2},{4,5},{5,4},{6,7},{7,6},{8,9},{9,8},{10,11... | collective-permute-start | bytes 1572872 | tf_op jit(solution)/shard_map/ppermute | solution.py:53
  40.3 0.0 collective-permute-done.2
  40.3 8.4 %collective-permute-done.3 = bf16[2,32,16,256]{3,2,1,0:T(8,128)(2,1)S(1)} collective-permute-done((bf16[2,32,16,256]{3,2,1,0:T(8,128)(2,1)S(1)}, bf16[2,32,16,256]{3,2,1,0:T(8,128)(2,1)S(1)}, u32[]{:S(2)}, u32[]{:S(2)}) %collective-permute-start.3) | collective-permute-done | bytes 524320 | tf_op jit(solution)/shard_map/ppermute | solution.py:55
  48.7 0.1 broadcast_select_fusion
  48.7 0.0 copy-start
  48.7 11.2 %collective-permute-done = bf16[2,32,16,256]{3,2,1,0:T(8,128)(2,1)S(1)} collective-permute-done((bf16[2,32,16,256]{3,2,1,0:T(8,128)(2,1)S(1)}, bf16[2,32,16,256]{3,2,1,0:T(8,128)(2,1)S(1)}, u32[]{:S(2)}, u32[]{:S(2)}) %collective-permute-start) | collective-permute-done | bytes 524320 | tf_op jit(solution)/shard_map/ppermute | solution.py:53
  59.9 0.3 pad_maximum_fusion
  60.2 0.0 copy-done
  60.2 0.5 fusion.3
  60.7 0.5 fusion.5
  61.2 0.6 fusion.13
  61.8 0.6 select_convert_fusion
  62.4 4.4 %collective-permute-start.4 = (bf16[32,64,128]{2,1,0:T(8,128)(2,1)S(1)}, bf16[32,64,128]{2,1,0:T(8,128)(2,1)S(1)}, u32[]{:S(2)}, u32[]{:S(2)}) collective-permute-start(bf16[32,64,128]{2,1,0:T(8,128)(2,1)S(1)} %get-tuple-element.9), channel_id=1, source_target_pairs={{0,4},{4,0},{1,5},{5,1},{2,6},{6,2},{3,7},{7,3},{8,12},{12,8},{9,1... | collective-permute-start | bytes 1572872 | tf_op jit(solution)/shard_map/ppermute | solution.py:66
  66.8 1.5 %collective-permute-done.4 = bf16[32,64,128]{2,1,0:T(8,128)(2,1)S(1)} collective-permute-done((bf16[32,64,128]{2,1,0:T(8,128)(2,1)S(1)}, bf16[32,64,128]{2,1,0:T(8,128)(2,1)S(1)}, u32[]{:S(2)}, u32[]{:S(2)}) %collective-permute-start.4) | collective-permute-done | bytes 524320 | tf_op jit(solution)/shard_map/ppermute | solution.py:66
  68.3 0.3 add_convert_fusion
  68.6 0.0 copy-start.3
  68.6 0.0 copy-start.2
  68.7 0.0 copy-start.1
  68.7 18.0 %all_to_all.10 = bf16[16,2,64,128]{3,2,1,0:T(8,128)(2,1)S(1)} all-to-all(bf16[16,2,64,128]{3,2,1,0:T(8,128)(2,1)S(1)} %bitcast.62), channel_id=1, replica_groups=mesh['y'=4,'zh'=2,'x'=4,'core'=2,'q'=4] {'y','x'}, dimensions={0} | all-to-all | bytes 1048576 | tf_op jit(solution)/shard_map/all_to_all | solution.py:73
  86.7 0.1 convert_reduce_fusion
  86.8 0.7 broadcast_in_dim.24
  87.5 7.8 %all-to-all-start.1 = ((f32[8,64,128]{2,1,0:T(8,128)}), f32[8,64,128]{2,1,0:T(8,128)S(1)}, u32[]{:S(2)}, u32[]{:S(2)}) async-start(f32[8,64,128]{2,1,0:T(8,128)} %bitcast.10), calls=%async_computation.1 | async-start | bytes 524288 | tf_op jit(solution)/shard_map/all_to_all | solution.py:78
  95.3 9.2 %all-to-all-done.1 = f32[8,64,128]{2,1,0:T(8,128)S(1)} async-done(((f32[8,64,128]{2,1,0:T(8,128)}), f32[8,64,128]{2,1,0:T(8,128)S(1)}, u32[]{:S(2)}, u32[]{:S(2)}) %all-to-all-start.1) | async-done | bytes 262176 | tf_op jit(solution)/shard_map/all_to_all | solution.py:78
  104.5 0.6 gather_fusion
  105.1 0.0 copy-done.3
  105.1 0.6 gather_fusion.1
  105.6 0.0 copy-done.2
  105.6 0.6 gather_fusion.2
  106.2 0.0 copy-done.1
  106.2 0.6 gather_fusion.3
  106.8 0.1 pad_maximum_fusion.1
  106.9 3.7 %collective-permute-start.5 = (f32[4,64,128]{2,0,1:T(4,128)S(1)}, f32[4,64,128]{2,0,1:T(4,128)S(1)}, u32[]{:S(2)}, u32[]{:S(2)}) collective-permute-start(f32[4,64,128]{2,0,1:T(4,128)S(1)} %pad_maximum_fusion.1), channel_id=1, source_target_pairs={{0,4},{4,0},{1,5},{5,1},{2,6},{6,2},{3,7},{7,3},{8,12},{12,8},{9,1... | collective-permute-start | bytes 393224 | tf_op jit(solution)/shard_map/ppermute | solution.py:84
  110.7 1.0 collective-permute-done.5
  111.7 0.1 broadcast_select_fusion.1
  112.0 0.3 fusion.20
  112.3 0.3 fusion.19
  112.6 0.7 maximum_bitcast_fusion
  (11 shorter events, 0.3 us)
Async XLA Ops:
  10.7 26.1 %collective-permute-start.1 = (bf16[2,32,16,256]{3,2,1,0:T(8,128)(2,1)S(1)}, bf16[2,32,16,256]{3,2,1,0:T(8,128)(2,1)S(1)}, u32[]{:S(2)}, u32[]{:S(2)}) collective-permute-start(bf16[2,32,16,256]{3,2,1,0:T(8,128)(2,1)S(1)} %bitcast.64), channel_id=1, source_target_pairs={{0,2},{2,0},{1,3},{3,1},{4,6},{6,4},{5,7},{7,5},{8,10},{10,8},{9,1... | collective-permute-start | bytes 1572872 | tf_op jit(solution)/shard_map/ppermute | solution.py:52
  14.6 25.7 %collective-permute-start.2 = (bf16[2,32,16,256]{3,2,1,0:T(8,128)(2,1)S(1)}, bf16[2,32,16,256]{3,2,1,0:T(8,128)(2,1)S(1)}, u32[]{:S(2)}, u32[]{:S(2)}) collective-permute-start(bf16[2,32,16,256]{3,2,1,0:T(8,128)(2,1)S(1)} %bitcast.65), channel_id=1, source_target_pairs={{1,2},{2,1},{5,6},{6,5},{9,10},{10,9},{13,14},{14,13},{17,18},{18,... | collective-permute-start | bytes 1572872 | tf_op jit(solution)/shard_map/ppermute | solution.py:54
  36.8 11.9 %collective-permute-start.3 = (bf16[2,32,16,256]{3,2,1,0:T(8,128)(2,1)S(1)}, bf16[2,32,16,256]{3,2,1,0:T(8,128)(2,1)S(1)}, u32[]{:S(2)}, u32[]{:S(2)}) collective-permute-start(bf16[2,32,16,256]{3,2,1,0:T(8,128)(2,1)S(1)} %collective-permute-done.1), channel_id=1, source_target_pairs={{2,3},{1,0},{6,7},{5,4},{10,11},{9,8},{14,15},{13,12},{18,19},{17,... | collective-permute-start | bytes 1572872 | tf_op jit(solution)/shard_map/ppermute | solution.py:55
  38.1 21.8 %collective-permute-start = (bf16[2,32,16,256]{3,2,1,0:T(8,128)(2,1)S(1)}, bf16[2,32,16,256]{3,2,1,0:T(8,128)(2,1)S(1)}, u32[]{:S(2)}, u32[]{:S(2)}) collective-permute-start(bf16[2,32,16,256]{3,2,1,0:T(8,128)(2,1)S(1)} %bitcast.66), channel_id=1, source_target_pairs={{0,1},{1,0},{2,3},{3,2},{4,5},{5,4},{6,7},{7,6},{8,9},{9,8},{10,11... | collective-permute-start | bytes 1572872 | tf_op jit(solution)/shard_map/ppermute | solution.py:53
  48.7 11.5 %copy-start = (bf16[2,32,256,128]{3,2,1,0:T(8,128)(2,1)S(1)}, bf16[2,32,256,128]{3,2,1,0:T(8,128)(2,1)}, u32[]{:S(2)}) copy-start(bf16[2,32,256,128]{3,2,1,0:T(8,128)(2,1)} %param.8) | copy-start | bytes 12582916
  62.4 6.0 %collective-permute-start.4 = (bf16[32,64,128]{2,1,0:T(8,128)(2,1)S(1)}, bf16[32,64,128]{2,1,0:T(8,128)(2,1)S(1)}, u32[]{:S(2)}, u32[]{:S(2)}) collective-permute-start(bf16[32,64,128]{2,1,0:T(8,128)(2,1)S(1)} %get-tuple-element.9), channel_id=1, source_target_pairs={{0,4},{4,0},{1,5},{5,1},{2,6},{6,2},{3,7},{7,3},{8,12},{12,8},{9,1... | collective-permute-start | bytes 1572872 | tf_op jit(solution)/shard_map/ppermute | solution.py:66
  68.6 36.4 %copy-start.3 = (s32[4]{0:T(128)S(1)}, s32[4]{0:T(128)}, u32[]{:S(2)}) copy-start(s32[4]{0:T(128)} %constant.159) | copy-start | bytes 52
  68.6 37.0 %copy-start.2 = (s32[4]{0:T(128)S(1)}, s32[4]{0:T(128)}, u32[]{:S(2)}) copy-start(s32[4]{0:T(128)} %constant.167) | copy-start | bytes 52
  68.7 37.6 %copy-start.1 = (s32[4]{0:T(128)S(1)}, s32[4]{0:T(128)}, u32[]{:S(2)}) copy-start(s32[4]{0:T(128)} %constant.175) | copy-start | bytes 52
  87.5 17.0 %all-to-all-start.1 = ((f32[8,64,128]{2,1,0:T(8,128)}), f32[8,64,128]{2,1,0:T(8,128)S(1)}, u32[]{:S(2)}, u32[]{:S(2)}) async-start(f32[8,64,128]{2,1,0:T(8,128)} %bitcast.10), calls=%async_computation.1 | async-start | bytes 524288 | tf_op jit(solution)/shard_map/all_to_all | solution.py:78
  106.9 4.7 %collective-permute-start.5 = (f32[4,64,128]{2,0,1:T(4,128)S(1)}, f32[4,64,128]{2,0,1:T(4,128)S(1)}, u32[]{:S(2)}, u32[]{:S(2)}) collective-permute-start(f32[4,64,128]{2,0,1:T(4,128)S(1)} %pad_maximum_fusion.1), channel_id=1, source_target_pairs={{0,4},{4,0},{1,5},{5,1},{2,6},{6,2},{3,7},{7,3},{8,12},{12,8},{9,1... | collective-permute-start | bytes 393224 | tf_op jit(solution)/shard_map/ppermute | solution.py:84

commit v2 on v1

v2 whole, which is shorter than its diff:
```python
import functools
import math

import jax
import jax.numpy as jnp
from jax import lax
from jax.experimental import pallas as pl
from jax.experimental.pallas import tpu as pltpu
from jax.sharding import Mesh, PartitionSpec as P

AXES = ("y", "zh", "x", "core", "q")
NEAR = [(0, 1), (1, 0), (2, 3), (3, 2)]
MIDDLE = [(1, 2), (2, 1)]
OUT = [(2, 3), (1, 0)]
SWAP = [(0, 1), (1, 0)]


def cosine(ticks, length):
    left = length // 4 - jnp.minimum(ticks, length - ticks)
    angle = left.astype(jnp.float32) * (2.0 * math.pi / length)
    square = angle * angle
    value = jnp.float32(-1.0 / math.factorial(11))
    for k in (9, 7, 5, 3, 1):
        value = value * square + (-1.0) ** (k // 2) / math.factorial(k)
    return value * angle


def dft_table(bins, length):
    chans = bins.shape[0]
    lanes = 128
    row = lax.broadcasted_iota(jnp.int32, (2 * chans, lanes), 0)
    turns = jnp.zeros((2 * chans, lanes), jnp.int32)
    for c in range(chans):
        turns = jnp.where(row % chans == c, bins[c], turns)
    turns = jnp.concatenate([turns] * (length // lanes), axis=1)
    clock_ticks = lax.broadcasted_iota(jnp.int32, turns.shape, 1)
    quarter = jnp.where(lax.broadcasted_iota(jnp.int32, turns.shape, 0) >= chans, length // 4, 0)
    turned = (clock_ticks * turns + quarter) & (length - 1)
    hann_envelope = 0.5 - 0.5 * cosine(clock_ticks, length)
    return (hann_envelope / math.sqrt(length) * cosine(turned, length)).astype(jnp.bfloat16)


def spectra_kernel(part, steps, bins_in, samples, out, held, rows, turned, bins, sems, bins_sem):
    sensors, snaps, ticks = held.shape
    columns = 2 * bins.shape[0]
    block = sensors // steps
    bins_copy = pltpu.make_async_copy(bins_in, bins, bins_sem)
    bins_copy.start()
    copies = []
    for i in range(steps):
        copy = pltpu.make_async_copy(
            samples.at[pl.ds(part * sensors + i * block, block)],
            held.at[pl.ds(i * block, block)],
            sems.at[i],
        )
        copy.start()
        copies.append(copy)
    bins_copy.wait()
    table = dft_table(bins, ticks)
    half = block // 2
    for i in range(steps):
        copies[i].wait()
        for j in range(2):
            first = i * block + j * half
            rows[pl.ds(first * snaps, half * snaps), :columns] = lax.dot_general(
                held[pl.ds(first, half)].reshape(half * snaps, ticks),
                table,
                (((1,), (1,)), ((), ())),
                preferred_element_type=jnp.float32,
            )
    for n in range(snaps):
        one = rows[pl.ds(n, sensors, stride=snaps), :].T[:columns]
        turned[pl.ds(n, columns, stride=snaps), :] = one
    out[...] = turned[...].astype(jnp.bfloat16).reshape(out.shape)


def spectra_of(samples, bins, part, parts):
    sensors, snaps, ticks = samples.shape
    sensors = sensors // parts
    columns = 2 * bins.shape[0]
    steps = 4
    return pl.pallas_call(
        functools.partial(spectra_kernel, part, steps),
        out_shape=jax.ShapeDtypeStruct((columns, snaps, sensors), jnp.bfloat16),
        in_specs=[pl.BlockSpec(memory_space=pl.ANY)] * 2,
        out_specs=pl.BlockSpec(memory_space=pltpu.VMEM),
        scratch_shapes=[
            pltpu.VMEM((sensors, snaps, ticks), jnp.bfloat16),
            pltpu.VMEM((sensors * snaps, 128), jnp.float32),
            pltpu.VMEM((columns * snaps, sensors), jnp.float32),
            pltpu.SMEM(bins.shape, bins.dtype),
            pltpu.SemaphoreType.DMA((steps,)),
            pltpu.SemaphoreType.DMA(()),
        ],
        compiler_params=pltpu.CompilerParams(vmem_limit_bytes=55 * 2**20),
        cost_estimate=pl.CostEstimate(
            flops=2 * sensors * snaps * ticks * columns,
            bytes_accessed=2 * sensors * snaps * (ticks + columns),
            transcendentals=0,
        ),
        name="spectra",
    )(bins, samples)


def load_kernel(weights, out, sems):
    beams = weights.shape[3]
    copies = []
    for part in range(2):
        for i in range(2):
            half = weights.shape[1] // 2
            channels = pl.ds(i * half, half)
            copy = pltpu.make_async_copy(
                weights.at[part, channels],
                out.at[channels, :, pl.ds(part * beams, beams)],
                sems.at[part, i],
            )
            copy.start()
            copies.append(copy)
    for copy in copies:
        copy.wait()


def load(weights):
    _, chans, sensors, beams = weights.shape
    return pl.pallas_call(
        load_kernel,
        out_shape=jax.ShapeDtypeStruct((chans, sensors, 2 * beams), weights.dtype),
        in_specs=[pl.BlockSpec(memory_space=pl.ANY)],
        out_specs=pl.BlockSpec(memory_space=pltpu.VMEM),
        scratch_shapes=[pltpu.SemaphoreType.DMA((2, 2))],
        compiler_params=pltpu.CompilerParams(vmem_limit_bytes=48 * 2**20),
        cost_estimate=pl.CostEstimate(
            flops=0, bytes_accessed=2 * weights.size * 2, transcendentals=0
        ),
        name="load",
    )(weights)


def beams_kernel(place, *refs):
    weights, keep, send = refs[-3:]
    own, near, middle, out, middle_2, out_2 = [refs[2 * k : 2 * k + 2] for k in range(6)]
    second = place[1] == 1
    orders = (
        (own, near, out, out_2),
        (near, own, middle, middle_2),
        (middle_2, middle, own, near),
        (out_2, out, near, own),
    )

    def run(order):
        def one_channel(ch, _):
            left = []
            for part in range(2):
                for one, two in order:
                    left.append(jnp.concatenate([one[part, ch], two[part, ch]], axis=1))
            left = jnp.concatenate(left, axis=0)
            both = jnp.dot(left, weights[ch], preferred_element_type=jnp.float32)
            half, beams = both.shape[0] // 2, both.shape[1] // 2
            real_y = both[:half, :beams] - both[half:, beams:]
            imag_y = both[:half, beams:] + both[half:, :beams]
            to = (ch // 8 * 4 + ch % 4, ch // 4 % 2)
            keep[to] = jnp.where(second, imag_y, real_y)
            send[to] = jnp.where(second, real_y, imag_y).astype(jnp.bfloat16)
            return 0

        lax.fori_loop(0, weights.shape[0], one_channel, 0, unroll=8)

    for q in range(4):
        pl.when(place[0] == q)(functools.partial(run, orders[q]))


def partial_beams(place, blocks, weights):
    _, chans, snaps, sensors = blocks[0].shape
    beams = weights.shape[2] // 2
    shape = (chans // 2, 2, 4 * snaps, beams)
    return pl.pallas_call(
        beams_kernel,
        out_shape=[
            jax.ShapeDtypeStruct(shape, jnp.float32),
            jax.ShapeDtypeStruct(shape, jnp.bfloat16),
        ],
        in_specs=[pl.BlockSpec(memory_space=pltpu.SMEM)]
        + [pl.BlockSpec(memory_space=pltpu.VMEM)] * (len(blocks) + 1),
        out_specs=[pl.BlockSpec(memory_space=pltpu.VMEM)] * 2,
        compiler_params=pltpu.CompilerParams(vmem_limit_bytes=32 * 2**20),
        name="beams",
    )(place, *blocks, weights)


def gram_kernel(place, mine, other, out):
    q, core = place[0], place[1]
    snaps = mine.shape[2]
    whole = []
    for part in range(2):
        blocks = []
        for b in range(4):
            ours = mine[0, b].astype(jnp.float32) + mine[1, b].astype(jnp.float32)
            theirs = other[0, b].astype(jnp.float32) + other[1, b].astype(jnp.float32)
            blocks.append(jnp.where(core == part, ours, theirs))
        whole.append(blocks)
    real_y, imag_y = whole

    def row(a):
        low = jnp.where(q % 2 == 0, a[0], a[1])
        high = jnp.where(q % 2 == 0, a[2], a[3])
        return jnp.where(q < 2, low, high)

    def columns(a):
        return jnp.concatenate(
            [jnp.where(core == 0, a[0], a[2]), jnp.where(core == 0, a[1], a[3])], axis=1
        )

    left_real, left_imag = row(real_y), row(imag_y)
    right = jnp.concatenate([columns(real_y), columns(imag_y)], axis=0)
    inverse = 1.0 / snaps

    def contract(left):
        return lax.dot_general(
            left,
            right,
            (((0,), (0,)), ((), ())),
            precision=lax.Precision.HIGHEST,
            preferred_element_type=jnp.float32,
        )

    out[0, 0] = contract(jnp.concatenate([left_real, left_imag], axis=0)) * inverse
    out[1, 0] = contract(jnp.concatenate([left_imag, -left_real], axis=0)) * inverse


def gram(place, mine, other):
    beams = mine.shape[3]
    return pl.pallas_call(
        gram_kernel,
        out_shape=jax.ShapeDtypeStruct((2, 1, beams, 2 * beams), jnp.float32),
        in_specs=[
            pl.BlockSpec(memory_space=pltpu.SMEM),
            pl.BlockSpec(memory_space=pltpu.VMEM),
            pl.BlockSpec(memory_space=pltpu.VMEM),
        ],
        out_specs=pl.BlockSpec(memory_space=pltpu.VMEM),
        compiler_params=pltpu.CompilerParams(vmem_limit_bytes=32 * 2**20),
        name="gram",
    )(place, mine, other)


def local(samples, weights, chosen_frequency_bins):
    chans = chosen_frequency_bins.shape[0]
    place = jnp.stack([lax.axis_index("q"), lax.axis_index("core")]).astype(jnp.int32)
    own = [spectra_of(samples, chosen_frequency_bins, part, 2) for part in range(2)]
    own = [x.reshape(2, chans, *x.shape[1:]) for x in own]

    def pass_on(pieces, pairs):
        return [lax.ppermute(x, "q", pairs) for x in pieces]

    def after(piece, other):
        return lax.optimization_barrier((piece, other))[0]

    near = pass_on(own, NEAR)
    middle = pass_on(own, MIDDLE)
    out = pass_on(middle, OUT)
    middle_2 = pass_on(near, MIDDLE)
    out_2 = pass_on(middle_2, OUT)
    weights = load(after(weights, middle[0]))
    blocks = own + near + middle + out + middle_2 + out_2
    keep, send = partial_beams(place, blocks, weights)
    theirs = lax.ppermute(send, "core", SWAP)
    mine = (keep + theirs.astype(jnp.float32)).astype(jnp.bfloat16)
    mine = lax.all_to_all(mine, ("y", "x"), 0, 0)
    mine = jnp.sum(mine.astype(jnp.float32), axis=0).astype(jnp.bfloat16)
    mine = jnp.broadcast_to(mine[:, None], (2, 4, *mine.shape[1:]))
    mine = mine.reshape(8, *mine.shape[2:])
    mine = lax.all_to_all(mine, ("zh", "q"), 0, 0)
    mine = mine.reshape(2, 4, *mine.shape[1:])
    other = lax.ppermute(mine, "core", SWAP)
    return gram(place, mine, other)


def solution(mesh):
    fine = Mesh(mesh.devices.reshape(4, 2, 4, 2, 4), AXES)
    sens = ("y", "zh", "x", "core")
    return jax.shard_map(
        local,
        mesh=fine,
        in_specs=(P(sens, "q", None), P(None, None, sens, "q"), P()),
        out_specs=P(None, sens, "q", None),
        check_vma=False,
    )
```

time: 114 us -> 90.5 us (0.79)
  waiting for transfers between devices: 52.7 us -> 27.9 us
  blocking collectives: 18 us -> 32 us
  Pallas kernels: 0 us -> 13.9 us
  matrix products: 8.79 us -> 0 us
  starting transfers between devices: 24.1 us -> 15.8 us
  local copies, waits for them, and re-layouts: 6.5 us -> 0.03 us
  other arithmetic: 3.02 us -> 0.31 us
    ppermute x5 -> x11, waiting for transfers between devices: 42.6 us -> 26.9 us  [the longest x10 25.4 us: pass_on(): return [lax.ppermute(x, 'q', pairs) for x in pieces]]
    all_to_all x0 -> x1, blocking collectives: none -> 14.7 us  [local(): mine = lax.all_to_all(mine, ('zh', 'q'), 0, 0)]
    pallas_call x0 -> x5, Pallas kernels: none -> 13.9 us  [the longest x2 8.16 us: spectra_of(): pl.pallas_call(functools.partial(spectra_kernel, part, steps), out_shape=...]
    all_to_all x1 -> x0, waiting for transfers between devices: 9.19 us -> none  [local(): lax.all_to_all(mine, ('zh', 'q'), 0, 0).reshape(2, 4, snaps, beams_local)]
    dot_general x7 -> x0, matrix products: 8.79 us -> none  [the longest x1 6.04 us: local(): jnp.dot(samples.reshape(sens_local * snap_local, fourier_length), table,...]
    all_to_all x1 -> x0, starting transfers between devices: 7.8 us -> none  [local(): lax.all_to_all(mine, ('zh', 'q'), 0, 0).reshape(2, 4, snaps, beams_local)]
    reshape x2 -> x0, local copies, waits for them, and re-layouts: 2.85 us -> none  [local(): spectra.reshape(sens_local, snap_local, 2, chans).transpose(2, 3, 1, 0)]
    gather x4 -> x0, local copies, waits for them, and re-layouts: 2.24 us -> none  [local(): mine[b, jnp.array([k ^ b for k in range(4)])]]
  transfers between devices with their start and end apart: 7 -> 12, of which waited for: 6 -> 7; matrix products, arithmetic and copies ran while one was open for 0% -> 0% of each run, Pallas kernels for 0% -> 7%
where the time goes in v2:
time: 90.5 us; the launch traced here: 90.2 us
  blocking collectives  32 us (35%)
  waiting for transfers between devices  27.9 us (31%)
  starting transfers between devices  15.8 us (17%)
  Pallas kernels  13.9 us (15%)
    ppermute x10, waiting for transfers between devices, pass_on(): return [lax.ppermute(x, 'q', pairs) for x in pieces]  25.4 us
    all_to_all x1, blocking collectives, local(): mine = lax.all_to_all(mine, ('y', 'x'), 0, 0)  17.3 us
    all_to_all x1, blocking collectives, local(): mine = lax.all_to_all(mine, ('zh', 'q'), 0, 0)  14.7 us
    ppermute x10, starting transfers between devices, pass_on(): return [lax.ppermute(x, 'q', pairs) for x in pieces]  10.5 us
    pallas_call x2, Pallas kernels, spectra_of(): pl.pallas_call(functools.partial(spectra_kernel, part, steps), out_shape=...  8.16 us
    ppermute x1, starting transfers between devices, local(): other = lax.ppermute(mine, 'core', SWAP)  3.11 us
    pallas_call x1, Pallas kernels, load(): pl.pallas_call(load_kernel, out_shape=jax.ShapeDtypeStruct((chans, sensor...  2.25 us
    ppermute x1, starting transfers between devices, local(): theirs = lax.ppermute(send, 'core', SWAP)  2.22 us
  transfers between devices with their start and end apart: 12, of which 7 were waited for; matrix products, arithmetic and copies ran while one was open for 0% of the time, Pallas kernels for 7%

profile of v2, /device:TPU:1, one launch (start us, length us, event | category | flops | bytes accessed | tf_op | source)
XLA Modules:
  0.0 90.2 jit_solution(9834114026103038348)
XLA Ops:
  0.0 4.1 %spectra.2 = bf16[64,16,128]{2,1,0:T(8,128)(2,1)} custom-call(s32[32]{0:T(128)} %bins_in.3, bf16[256,16,1024]{2,1,0:T(8,128)(2,1)} %samples.3), custom_call_target="tpu_custom_call" | custom-call | flops 268435456 | bytes 4456448 | tf_op jit(solution)/shard_map/spectra/pallas_call | solution.py:82
  4.1 0.0 copy-start
  4.1 2.6 %collective-permute-start = (bf16[2,32,16,128]{3,2,1,0:T(8,128)(2,1)}, bf16[2,32,16,128]{3,2,1,0:T(8,128)(2,1)S(1)}, u32[]{:S(2)}, u32[]{:S(2)}) collective-permute-start(bf16[2,32,16,128]{3,2,1,0:T(8,128)(2,1)} %bitcast.6), channel_id=1, source_target_pairs={{0,1},{1,0},{2,3},{3,2},{4,5},{5,4},{6,7},{7,6},{8,9},{9,8},{10,11... | collective-permute-start | bytes 786440 | tf_op jit(solution)/shard_map/ppermute | solution.py:253
  6.7 4.1 %spectra.3 = bf16[64,16,128]{2,1,0:T(8,128)(2,1)} custom-call(s32[32]{0:T(128)} %bins_in.3, bf16[256,16,1024]{2,1,0:T(8,128)(2,1)} %samples.3), custom_call_target="tpu_custom_call" | custom-call | flops 268435456 | bytes 4456448 | tf_op jit(solution)/shard_map/spectra/pallas_call | solution.py:82
  10.7 0.1 collective-permute-start.1
  10.8 0.0 copy-done
  10.9 0.7 collective-permute-start.2
  11.5 0.7 collective-permute-start.3
  12.2 0.0 collective-permute-done.refs_2_
  12.2 0.7 collective-permute-start.6
  12.9 5.0 %collective-permute-done.1.refs_3_ = bf16[2,32,16,128]{3,2,1,0:T(8,128)(2,1)S(1)} collective-permute-done((bf16[2,32,16,128]{3,2,1,0:T(8,128)(2,1)}, bf16[2,32,16,128]{3,2,1,0:T(8,128)(2,1)S(1)}, u32[]{:S(2)}, u32[]{:S(2)}) %collective-permute-start.1) | collective-permute-done | bytes 262176 | tf_op jit(solution)/shard_map/ppermute | solution.py:253
  17.9 0.7 collective-permute-start.7
  18.6 0.0 collective-permute-done.2.refs_4_
  18.6 1.3 %collective-permute-start.4 = (bf16[2,32,16,128]{3,2,1,0:T(8,128)(2,1)S(1)}, bf16[2,32,16,128]{3,2,1,0:T(8,128)(2,1)S(1)}, u32[]{:S(2)}, u32[]{:S(2)}) collective-permute-start(bf16[2,32,16,128]{3,2,1,0:T(8,128)(2,1)S(1)} %collective-permute-done.2.refs_4_), channel_id=1, source_target_pairs={{2,3},{1,0},{6,7},{5,4},{10,11},{9,8},{14,15},{13,12},{18,19},{17,... | collective-permute-start | bytes 786440 | tf_op jit(solution)/shard_map/ppermute | solution.py:253
  19.9 0.0 collective-permute-done.3.refs_5_
  19.9 1.3 %collective-permute-start.5 = (bf16[2,32,16,128]{3,2,1,0:T(8,128)(2,1)S(1)}, bf16[2,32,16,128]{3,2,1,0:T(8,128)(2,1)S(1)}, u32[]{:S(2)}, u32[]{:S(2)}) collective-permute-start(bf16[2,32,16,128]{3,2,1,0:T(8,128)(2,1)S(1)} %collective-permute-done.3.refs_5_), channel_id=1, source_target_pairs={{2,3},{1,0},{6,7},{5,4},{10,11},{9,8},{14,15},{13,12},{18,19},{17,... | collective-permute-start | bytes 786440 | tf_op jit(solution)/shard_map/ppermute | solution.py:253
  21.2 0.0 collective-permute-done.6.refs_8_
  21.2 1.3 %collective-permute-start.8 = (bf16[2,32,16,128]{3,2,1,0:T(8,128)(2,1)S(1)}, bf16[2,32,16,128]{3,2,1,0:T(8,128)(2,1)S(1)}, u32[]{:S(2)}, u32[]{:S(2)}) collective-permute-start(bf16[2,32,16,128]{3,2,1,0:T(8,128)(2,1)S(1)} %collective-permute-done.6.refs_8_), channel_id=1, source_target_pairs={{2,3},{1,0},{6,7},{5,4},{10,11},{9,8},{14,15},{13,12},{18,19},{17,... | collective-permute-start | bytes 786440 | tf_op jit(solution)/shard_map/ppermute | solution.py:253
  22.5 0.0 collective-permute-done.7.refs_9_
  22.5 1.3 %collective-permute-start.9 = (bf16[2,32,16,128]{3,2,1,0:T(8,128)(2,1)S(1)}, bf16[2,32,16,128]{3,2,1,0:T(8,128)(2,1)S(1)}, u32[]{:S(2)}, u32[]{:S(2)}) collective-permute-start(bf16[2,32,16,128]{3,2,1,0:T(8,128)(2,1)S(1)} %collective-permute-done.7.refs_9_), channel_id=1, source_target_pairs={{2,3},{1,0},{6,7},{5,4},{10,11},{9,8},{14,15},{13,12},{18,19},{17,... | collective-permute-start | bytes 786440 | tf_op jit(solution)/shard_map/ppermute | solution.py:253
  23.8 0.1 pad_add_fusion.place
  23.9 0.0 copy-start.1
  23.9 2.2 %load.1.refs_12_ = bf16[32,256,256]{2,1,0:T(8,128)(2,1)S(1)} custom-call(bf16[2,32,256,128]{3,2,1,0:T(8,128)(2,1)} %weights), custom_call_target="tpu_custom_call" | custom-call | bytes 8388608 | tf_op jit(solution)/shard_map/load/pallas_call | solution.py:125
  26.1 3.0 %collective-permute-done.4.refs_6_ = bf16[2,32,16,128]{3,2,1,0:T(8,128)(2,1)S(1)} collective-permute-done((bf16[2,32,16,128]{3,2,1,0:T(8,128)(2,1)S(1)}, bf16[2,32,16,128]{3,2,1,0:T(8,128)(2,1)S(1)}, u32[]{:S(2)}, u32[]{:S(2)}) %collective-permute-start.4) | collective-permute-done | bytes 262176 | tf_op jit(solution)/shard_map/ppermute | solution.py:253
  29.2 6.1 %collective-permute-done.5.refs_7_ = bf16[2,32,16,128]{3,2,1,0:T(8,128)(2,1)S(1)} collective-permute-done((bf16[2,32,16,128]{3,2,1,0:T(8,128)(2,1)S(1)}, bf16[2,32,16,128]{3,2,1,0:T(8,128)(2,1)S(1)}, u32[]{:S(2)}, u32[]{:S(2)}) %collective-permute-start.5) | collective-permute-done | bytes 262176 | tf_op jit(solution)/shard_map/ppermute | solution.py:253
  35.3 5.6 %collective-permute-done.8.refs_10_ = bf16[2,32,16,128]{3,2,1,0:T(8,128)(2,1)S(1)} collective-permute-done((bf16[2,32,16,128]{3,2,1,0:T(8,128)(2,1)S(1)}, bf16[2,32,16,128]{3,2,1,0:T(8,128)(2,1)S(1)}, u32[]{:S(2)}, u32[]{:S(2)}) %collective-permute-start.8) | collective-permute-done | bytes 262176 | tf_op jit(solution)/shard_map/ppermute | solution.py:253
  40.9 5.6 %collective-permute-done.9.refs_11_ = bf16[2,32,16,128]{3,2,1,0:T(8,128)(2,1)S(1)} collective-permute-done((bf16[2,32,16,128]{3,2,1,0:T(8,128)(2,1)S(1)}, bf16[2,32,16,128]{3,2,1,0:T(8,128)(2,1)S(1)}, u32[]{:S(2)}, u32[]{:S(2)}) %collective-permute-start.9) | collective-permute-done | bytes 262176 | tf_op jit(solution)/shard_map/ppermute | solution.py:253
  46.5 0.0 copy-done.1
  46.5 1.8 %beams.1 = (f32[16,2,64,128]{3,2,1,0:T(8,128)S(1)}, bf16[16,2,64,128]{3,2,1,0:T(8,128)(2,1)S(1)}) custom-call(s32[2]{0:T(128)S(1)} %pad_add_fusion.place, bf16[2,32,16,128]{3,2,1,0:T(8,128)(2,1)S(1)} %bitcast.8, bf16[2,32,16,128]{3,2,1,0:T(8,128)(2,1)S(1)} %bitcast.11, bf16[2,32,16,128]{3,2,1,0:T(8,128)(2,1)S(1)} %collective-permute-done.refs_2_, ...), custom_call_target="tpu_custom_call" | custom-call | tf_op jit(solution)/shard_map/beams/pallas_call | solution.py:176
  48.4 2.2 %collective-permute-start.10 = (bf16[16,2,64,128]{3,2,1,0:T(8,128)(2,1)S(1)}, bf16[16,2,64,128]{3,2,1,0:T(8,128)(2,1)S(1)}, u32[]{:S(2)}, u32[]{:S(2)}) collective-permute-start(bf16[16,2,64,128]{3,2,1,0:T(8,128)(2,1)S(1)} %get-tuple-element.10), channel_id=1, source_target_pairs={{0,4},{4,0},{1,5},{5,1},{2,6},{6,2},{3,7},{7,3},{8,12},{12,8},{9,1... | collective-permute-start | bytes 1572872 | tf_op jit(solution)/shard_map/ppermute | solution.py:266
  50.6 1.5 %collective-permute-done.10 = bf16[16,2,64,128]{3,2,1,0:T(8,128)(2,1)S(1)} collective-permute-done((bf16[16,2,64,128]{3,2,1,0:T(8,128)(2,1)S(1)}, bf16[16,2,64,128]{3,2,1,0:T(8,128)(2,1)S(1)}, u32[]{:S(2)}, u32[]{:S(2)}) %collective-permute-start.10) | collective-permute-done | bytes 524320 | tf_op jit(solution)/shard_map/ppermute | solution.py:266
  52.1 0.2 add_convert_fusion
  52.3 17.3 %all_to_all.10 = bf16[16,2,64,128]{3,2,1,0:T(8,128)(2,1)S(1)} all-to-all(bf16[16,2,64,128]{3,2,1,0:T(8,128)(2,1)S(1)} %add_convert_fusion), channel_id=1, replica_groups=mesh['y'=4,'zh'=2,'x'=4,'core'=2,'q'=4] {'y','x'}, dimensions={0} | all-to-all | bytes 1048576 | tf_op jit(solution)/shard_map/all_to_all | solution.py:268
  69.6 0.1 reduce_sum.12
  69.7 14.7 %all_to_all.11 = bf16[8,64,128]{2,1,0:T(8,128)(2,1)S(1)} all-to-all(bf16[8,64,128]{2,1,0:T(8,128)(2,1)S(1)} %bitcast.14), channel_id=1, replica_groups=mesh['y'=4,'zh'=2,'x'=4,'core'=2,'q'=4] {'zh','q'}, dimensions={0} | all-to-all | bytes 262144 | tf_op jit(solution)/shard_map/all_to_all | solution.py:272
  84.4 3.1 %collective-permute-start.11 = (bf16[2,4,64,128]{3,2,1,0:T(8,128)(2,1)S(1)}, bf16[2,4,64,128]{3,2,1,0:T(8,128)(2,1)S(1)}, u32[]{:S(2)}, u32[]{:S(2)}) collective-permute-start(bf16[2,4,64,128]{3,2,1,0:T(8,128)(2,1)S(1)} %bitcast.12), channel_id=1, source_target_pairs={{0,4},{4,0},{1,5},{5,1},{2,6},{6,2},{3,7},{7,3},{8,12},{12,8},{9,1... | collective-permute-start | bytes 393224 | tf_op jit(solution)/shard_map/ppermute | solution.py:274
  87.5 1.0 %collective-permute-done.11.other = bf16[2,4,64,128]{3,2,1,0:T(8,128)(2,1)S(1)} collective-permute-done((bf16[2,4,64,128]{3,2,1,0:T(8,128)(2,1)S(1)}, bf16[2,4,64,128]{3,2,1,0:T(8,128)(2,1)S(1)}, u32[]{:S(2)}, u32[]{:S(2)}) %collective-permute-start.11) | collective-permute-done | bytes 131104 | tf_op jit(solution)/shard_map/ppermute | solution.py:274
  88.5 1.7 %gram.1 = f32[2,1,128,256]{3,2,1,0:T(8,128)} custom-call(s32[2]{0:T(128)S(1)} %pad_add_fusion.place, bf16[2,4,64,128]{3,2,1,0:T(8,128)(2,1)S(1)} %bitcast.13, bf16[2,4,64,128]{3,2,1,0:T(8,128)(2,1)S(1)} %collective-permute-done.11.other), custom_call_target="tpu_custom_call" | custom-call | tf_op jit(solution)/shard_map/gram/pallas_call | solution.py:232
  (1 shorter events, 0.0 us)
Async XLA Ops:
  4.1 6.8 %copy-start = (bf16[64,16,128]{2,1,0:T(8,128)(2,1)S(1)}, bf16[64,16,128]{2,1,0:T(8,128)(2,1)}, u32[]{:S(2)}) copy-start(bf16[64,16,128]{2,1,0:T(8,128)(2,1)} %spectra.2) | copy-start | bytes 786436
  4.1 8.1 %collective-permute-start = (bf16[2,32,16,128]{3,2,1,0:T(8,128)(2,1)}, bf16[2,32,16,128]{3,2,1,0:T(8,128)(2,1)S(1)}, u32[]{:S(2)}, u32[]{:S(2)}) collective-permute-start(bf16[2,32,16,128]{3,2,1,0:T(8,128)(2,1)} %bitcast.6), channel_id=1, source_target_pairs={{0,1},{1,0},{2,3},{3,2},{4,5},{5,4},{6,7},{7,6},{8,9},{9,8},{10,11... | collective-permute-start | bytes 786440 | tf_op jit(solution)/shard_map/ppermute | solution.py:253
  10.7 7.2 %collective-permute-start.1 = (bf16[2,32,16,128]{3,2,1,0:T(8,128)(2,1)}, bf16[2,32,16,128]{3,2,1,0:T(8,128)(2,1)S(1)}, u32[]{:S(2)}, u32[]{:S(2)}) collective-permute-start(bf16[2,32,16,128]{3,2,1,0:T(8,128)(2,1)} %bitcast.9), channel_id=1, source_target_pairs={{0,1},{1,0},{2,3},{3,2},{4,5},{5,4},{6,7},{7,6},{8,9},{9,8},{10,11... | collective-permute-start | bytes 786440 | tf_op jit(solution)/shard_map/ppermute | solution.py:253
  10.9 7.7 %collective-permute-start.2 = (bf16[2,32,16,128]{3,2,1,0:T(8,128)(2,1)S(1)}, bf16[2,32,16,128]{3,2,1,0:T(8,128)(2,1)S(1)}, u32[]{:S(2)}, u32[]{:S(2)}) collective-permute-start(bf16[2,32,16,128]{3,2,1,0:T(8,128)(2,1)S(1)} %bitcast.7), channel_id=1, source_target_pairs={{1,2},{2,1},{5,6},{6,5},{9,10},{10,9},{13,14},{14,13},{17,18},{18,... | collective-permute-start | bytes 786440 | tf_op jit(solution)/shard_map/ppermute | solution.py:253
  11.5 8.3 %collective-permute-start.3 = (bf16[2,32,16,128]{3,2,1,0:T(8,128)(2,1)}, bf16[2,32,16,128]{3,2,1,0:T(8,128)(2,1)S(1)}, u32[]{:S(2)}, u32[]{:S(2)}) collective-permute-start(bf16[2,32,16,128]{3,2,1,0:T(8,128)(2,1)} %bitcast.10), channel_id=1, source_target_pairs={{1,2},{2,1},{5,6},{6,5},{9,10},{10,9},{13,14},{14,13},{17,18},{18,... | collective-permute-start | bytes 786440 | tf_op jit(solution)/shard_map/ppermute | solution.py:253
  12.2 9.0 %collective-permute-start.6 = (bf16[2,32,16,128]{3,2,1,0:T(8,128)(2,1)S(1)}, bf16[2,32,16,128]{3,2,1,0:T(8,128)(2,1)S(1)}, u32[]{:S(2)}, u32[]{:S(2)}) collective-permute-start(bf16[2,32,16,128]{3,2,1,0:T(8,128)(2,1)S(1)} %collective-permute-done.refs_2_), channel_id=1, source_target_pairs={{1,2},{2,1},{5,6},{6,5},{9,10},{10,9},{13,14},{14,13},{17,18},{18,... | collective-permute-start | bytes 786440 | tf_op jit(solution)/shard_map/ppermute | solution.py:253
  17.9 4.6 %collective-permute-start.7 = (bf16[2,32,16,128]{3,2,1,0:T(8,128)(2,1)S(1)}, bf16[2,32,16,128]{3,2,1,0:T(8,128)(2,1)S(1)}, u32[]{:S(2)}, u32[]{:S(2)}) collective-permute-start(bf16[2,32,16,128]{3,2,1,0:T(8,128)(2,1)S(1)} %collective-permute-done.1.refs_3_), channel_id=1, source_target_pairs={{1,2},{2,1},{5,6},{6,5},{9,10},{10,9},{13,14},{14,13},{17,18},{18,... | collective-permute-start | bytes 786440 | tf_op jit(solution)/shard_map/ppermute | solution.py:253
  18.6 10.6 %collective-permute-start.4 = (bf16[2,32,16,128]{3,2,1,0:T(8,128)(2,1)S(1)}, bf16[2,32,16,128]{3,2,1,0:T(8,128)(2,1)S(1)}, u32[]{:S(2)}, u32[]{:S(2)}) collective-permute-start(bf16[2,32,16,128]{3,2,1,0:T(8,128)(2,1)S(1)} %collective-permute-done.2.refs_4_), channel_id=1, source_target_pairs={{2,3},{1,0},{6,7},{5,4},{10,11},{9,8},{14,15},{13,12},{18,19},{17,... | collective-permute-start | bytes 786440 | tf_op jit(solution)/shard_map/ppermute | solution.py:253
  19.9 15.4 %collective-permute-start.5 = (bf16[2,32,16,128]{3,2,1,0:T(8,128)(2,1)S(1)}, bf16[2,32,16,128]{3,2,1,0:T(8,128)(2,1)S(1)}, u32[]{:S(2)}, u32[]{:S(2)}) collective-permute-start(bf16[2,32,16,128]{3,2,1,0:T(8,128)(2,1)S(1)} %collective-permute-done.3.refs_5_), channel_id=1, source_target_pairs={{2,3},{1,0},{6,7},{5,4},{10,11},{9,8},{14,15},{13,12},{18,19},{17,... | collective-permute-start | bytes 786440 | tf_op jit(solution)/shard_map/ppermute | solution.py:253
  21.2 19.7 %collective-permute-start.8 = (bf16[2,32,16,128]{3,2,1,0:T(8,128)(2,1)S(1)}, bf16[2,32,16,128]{3,2,1,0:T(8,128)(2,1)S(1)}, u32[]{:S(2)}, u32[]{:S(2)}) collective-permute-start(bf16[2,32,16,128]{3,2,1,0:T(8,128)(2,1)S(1)} %collective-permute-done.6.refs_8_), channel_id=1, source_target_pairs={{2,3},{1,0},{6,7},{5,4},{10,11},{9,8},{14,15},{13,12},{18,19},{17,... | collective-permute-start | bytes 786440 | tf_op jit(solution)/shard_map/ppermute | solution.py:253
  22.5 24.0 %collective-permute-start.9 = (bf16[2,32,16,128]{3,2,1,0:T(8,128)(2,1)S(1)}, bf16[2,32,16,128]{3,2,1,0:T(8,128)(2,1)S(1)}, u32[]{:S(2)}, u32[]{:S(2)}) collective-permute-start(bf16[2,32,16,128]{3,2,1,0:T(8,128)(2,1)S(1)} %collective-permute-done.7.refs_9_), channel_id=1, source_target_pairs={{2,3},{1,0},{6,7},{5,4},{10,11},{9,8},{14,15},{13,12},{18,19},{17,... | collective-permute-start | bytes 786440 | tf_op jit(solution)/shard_map/ppermute | solution.py:253
  23.9 22.6 %copy-start.1 = (bf16[64,16,128]{2,1,0:T(8,128)(2,1)S(1)}, bf16[64,16,128]{2,1,0:T(8,128)(2,1)}, u32[]{:S(2)}) copy-start(bf16[64,16,128]{2,1,0:T(8,128)(2,1)} %spectra.3) | copy-start | bytes 786436
  48.4 3.8 %collective-permute-start.10 = (bf16[16,2,64,128]{3,2,1,0:T(8,128)(2,1)S(1)}, bf16[16,2,64,128]{3,2,1,0:T(8,128)(2,1)S(1)}, u32[]{:S(2)}, u32[]{:S(2)}) collective-permute-start(bf16[16,2,64,128]{3,2,1,0:T(8,128)(2,1)S(1)} %get-tuple-element.10), channel_id=1, source_target_pairs={{0,4},{4,0},{1,5},{5,1},{2,6},{6,2},{3,7},{7,3},{8,12},{12,8},{9,1... | collective-permute-start | bytes 1572872 | tf_op jit(solution)/shard_map/ppermute | solution.py:266
  84.4 4.1 %collective-permute-start.11 = (bf16[2,4,64,128]{3,2,1,0:T(8,128)(2,1)S(1)}, bf16[2,4,64,128]{3,2,1,0:T(8,128)(2,1)S(1)}, u32[]{:S(2)}, u32[]{:S(2)}) collective-permute-start(bf16[2,4,64,128]{3,2,1,0:T(8,128)(2,1)S(1)} %bitcast.12), channel_id=1, source_target_pairs={{0,4},{4,0},{1,5},{5,1},{2,6},{6,2},{3,7},{7,3},{8,12},{12,8},{9,1... | collective-permute-start | bytes 393224 | tf_op jit(solution)/shard_map/ppermute | solution.py:274

commit v3 on v2

--- a/solution.py
+++ b/solution.py
@@ -11,6 +11,7 @@
 AXES = ("y", "zh", "x", "core", "q")
 NEAR = [(0, 1), (1, 0), (2, 3), (3, 2)]
 MIDDLE = [(1, 2), (2, 1)]
+FAR = [(0, 2), (2, 0), (1, 3), (3, 1)]
 OUT = [(2, 3), (1, 0)]
 SWAP = [(0, 1), (1, 0)]
 
@@ -138,13 +139,13 @@
 
 def beams_kernel(place, *refs):
     weights, keep, send = refs[-3:]
-    own, near, middle, out, middle_2, out_2 = [refs[2 * k : 2 * k + 2] for k in range(6)]
+    own, near, far, middle, out = [refs[2 * k : 2 * k + 2] for k in range(5)]
     second = place[1] == 1
     orders = (
-        (own, near, out, out_2),
-        (near, own, middle, middle_2),
-        (middle_2, middle, own, near),
-        (out_2, out, near, own),
+        (own, near, far, out),
+        (near, own, middle, far),
+        (far, middle, own, near),
+        (out, far, near, own),
     )
 
     def run(order):
@@ -194,8 +195,8 @@
     for part in range(2):
         blocks = []
         for b in range(4):
-            ours = mine[0, b].astype(jnp.float32) + mine[1, b].astype(jnp.float32)
-            theirs = other[0, b].astype(jnp.float32) + other[1, b].astype(jnp.float32)
+            ours = mine[b, 0].astype(jnp.float32) + mine[b, 1].astype(jnp.float32)
+            theirs = other[b, 0].astype(jnp.float32) + other[b, 1].astype(jnp.float32)
             blocks.append(jnp.where(core == part, ours, theirs))
         whole.append(blocks)
     real_y, imag_y = whole
@@ -255,22 +256,21 @@
     def after(piece, other):
         return lax.optimization_barrier((piece, other))[0]
 
+    far = pass_on(own, FAR)
     near = pass_on(own, NEAR)
-    middle = pass_on(own, MIDDLE)
-    out = pass_on(middle, OUT)
-    middle_2 = pass_on(near, MIDDLE)
-    out_2 = pass_on(middle_2, OUT)
-    weights = load(after(weights, middle[0]))
-    blocks = own + near + middle + out + middle_2 + out_2
+    out = pass_on(far, OUT)
+    middle = pass_on([after(x, far[0]) for x in own], MIDDLE)
+    weights = load(after(weights, far[-1]))
+    blocks = own + near + far + middle + out
     keep, send = partial_beams(place, blocks, weights)
     theirs = lax.ppermute(send, "core", SWAP)
     mine = (keep + theirs.astype(jnp.float32)).astype(jnp.bfloat16)
     mine = lax.all_to_all(mine, ("y", "x"), 0, 0)
     mine = jnp.sum(mine.astype(jnp.float32), axis=0).astype(jnp.bfloat16)
-    mine = jnp.broadcast_to(mine[:, None], (2, 4, *mine.shape[1:]))
+    mine = jnp.broadcast_to(mine[None], (4, 2, *mine.shape[1:]))
     mine = mine.reshape(8, *mine.shape[2:])
-    mine = lax.all_to_all(mine, ("zh", "q"), 0, 0)
-    mine = mine.reshape(2, 4, *mine.shape[1:])
+    mine = lax.all_to_all(mine, ("q", "zh"), 0, 0)
+    mine = mine.reshape(4, 2, *mine.shape[1:])
     other = lax.ppermute(mine, "core", SWAP)
     return gram(place, mine, other)
 

time: 90.5 us -> 84.9 us (0.938)
  waiting for transfers between devices: 27.9 us -> 23.7 us
    ppermute x10 -> x8, waiting for transfers between devices: 25.4 us -> 21.2 us  [pass_on(): return [lax.ppermute(x, 'q', pairs) for x in pieces]]
    ppermute x10 -> x8, starting transfers between devices: 10.5 us -> 9.66 us  [pass_on(): return [lax.ppermute(x, 'q', pairs) for x in pieces]]
  transfers between devices with their start and end apart: 12 -> 10, of which waited for: 7 -> 6; matrix products, arithmetic and copies ran while one was open for 0% -> 0% of each run, Pallas kernels for 7% -> 7%
where the time goes in v3:
time: 84.9 us; the launch traced here: 84.7 us
  blocking collectives  31.2 us (37%)
  waiting for transfers between devices  23.7 us (28%)
  starting transfers between devices  15.3 us (18%)
  Pallas kernels  13.9 us (16%)
    ppermute x8, waiting for transfers between devices, pass_on(): return [lax.ppermute(x, 'q', pairs) for x in pieces]  21.2 us
    all_to_all x1, blocking collectives, local(): mine = lax.all_to_all(mine, ('y', 'x'), 0, 0)  17.3 us
    all_to_all x1, blocking collectives, local(): mine = lax.all_to_all(mine, ('q', 'zh'), 0, 0)  13.9 us
    ppermute x8, starting transfers between devices, pass_on(): return [lax.ppermute(x, 'q', pairs) for x in pieces]  9.66 us
    pallas_call x2, Pallas kernels, spectra_of(): pl.pallas_call(functools.partial(spectra_kernel, part, steps), out_shape=...  8.17 us
    ppermute x1, starting transfers between devices, local(): other = lax.ppermute(mine, 'core', SWAP)  3.29 us
    ppermute x1, starting transfers between devices, local(): theirs = lax.ppermute(send, 'core', SWAP)  2.4 us
    pallas_call x1, Pallas kernels, load(): pl.pallas_call(load_kernel, out_shape=jax.ShapeDtypeStruct((chans, sensor...  2.25 us
  transfers between devices with their start and end apart: 10, of which 6 were waited for; matrix products, arithmetic and copies ran while one was open for 0% of the time, Pallas kernels for 7%

profile of v3, /device:TPU:1, one launch (start us, length us, event | category | flops | bytes accessed | tf_op | source)
XLA Modules:
  0.0 84.7 jit_solution(15459265928101788979)
XLA Ops:
  0.0 4.1 %spectra.2 = bf16[64,16,128]{2,1,0:T(8,128)(2,1)} custom-call(s32[32]{0:T(128)} %bins_in.3, bf16[256,16,1024]{2,1,0:T(8,128)(2,1)} %samples.3), custom_call_target="tpu_custom_call" | custom-call | flops 268435456 | bytes 4456448 | tf_op jit(solution)/shard_map/spectra/pallas_call | solution.py:83
  4.1 0.0 copy-start
  4.1 3.9 %collective-permute-start.2 = (bf16[2,32,16,128]{3,2,1,0:T(8,128)(2,1)}, bf16[2,32,16,128]{3,2,1,0:T(8,128)(2,1)S(1)}, u32[]{:S(2)}, u32[]{:S(2)}) collective-permute-start(bf16[2,32,16,128]{3,2,1,0:T(8,128)(2,1)} %bitcast.6), channel_id=1, source_target_pairs={{0,2},{2,0},{1,3},{3,1},{4,6},{6,4},{5,7},{7,5},{8,10},{10,8},{9,1... | collective-permute-start | bytes 786440 | tf_op jit(solution)/shard_map/ppermute | solution.py:254
  8.0 1.7 %collective-permute-start = (bf16[2,32,16,128]{3,2,1,0:T(8,128)(2,1)}, bf16[2,32,16,128]{3,2,1,0:T(8,128)(2,1)S(1)}, u32[]{:S(2)}, u32[]{:S(2)}) collective-permute-start(bf16[2,32,16,128]{3,2,1,0:T(8,128)(2,1)} %bitcast.7), channel_id=1, source_target_pairs={{0,1},{1,0},{2,3},{3,2},{4,5},{5,4},{6,7},{7,6},{8,9},{9,8},{10,11... | collective-permute-start | bytes 786440 | tf_op jit(solution)/shard_map/ppermute | solution.py:254
  9.6 4.1 %spectra.3 = bf16[64,16,128]{2,1,0:T(8,128)(2,1)} custom-call(s32[32]{0:T(128)} %bins_in.3, bf16[256,16,1024]{2,1,0:T(8,128)(2,1)} %samples.3), custom_call_target="tpu_custom_call" | custom-call | flops 268435456 | bytes 4456448 | tf_op jit(solution)/shard_map/spectra/pallas_call | solution.py:83
  13.7 0.2 collective-permute-start.3
  13.9 0.0 collective-permute-start.1
  13.9 5.3 %collective-permute-done.2.refs_4_ = bf16[2,32,16,128]{3,2,1,0:T(8,128)(2,1)S(1)} collective-permute-done((bf16[2,32,16,128]{3,2,1,0:T(8,128)(2,1)}, bf16[2,32,16,128]{3,2,1,0:T(8,128)(2,1)S(1)}, u32[]{:S(2)}, u32[]{:S(2)}) %collective-permute-start.2) | collective-permute-done | bytes 262176 | tf_op jit(solution)/shard_map/ppermute | solution.py:254
  19.2 0.0 copy-done
  19.2 0.7 collective-permute-start.4
  19.9 0.7 collective-permute-start.5
  20.6 0.0 collective-permute-done.refs_2_
  20.6 1.3 %collective-permute-start.6 = (bf16[2,32,16,128]{3,2,1,0:T(8,128)(2,1)S(1)}, bf16[2,32,16,128]{3,2,1,0:T(8,128)(2,1)S(1)}, u32[]{:S(2)}, u32[]{:S(2)}) collective-permute-start(bf16[2,32,16,128]{3,2,1,0:T(8,128)(2,1)S(1)} %collective-permute-done.2.refs_4_), channel_id=1, source_target_pairs={{2,3},{1,0},{6,7},{5,4},{10,11},{9,8},{14,15},{13,12},{18,19},{17,... | collective-permute-start | bytes 786440 | tf_op jit(solution)/shard_map/ppermute | solution.py:254
  21.9 8.6 %collective-permute-done.3.refs_5_ = bf16[2,32,16,128]{3,2,1,0:T(8,128)(2,1)S(1)} collective-permute-done((bf16[2,32,16,128]{3,2,1,0:T(8,128)(2,1)}, bf16[2,32,16,128]{3,2,1,0:T(8,128)(2,1)S(1)}, u32[]{:S(2)}, u32[]{:S(2)}) %collective-permute-start.3) | collective-permute-done | bytes 262176 | tf_op jit(solution)/shard_map/ppermute | solution.py:254
  30.5 1.3 %collective-permute-start.7 = (bf16[2,32,16,128]{3,2,1,0:T(8,128)(2,1)S(1)}, bf16[2,32,16,128]{3,2,1,0:T(8,128)(2,1)S(1)}, u32[]{:S(2)}, u32[]{:S(2)}) collective-permute-start(bf16[2,32,16,128]{3,2,1,0:T(8,128)(2,1)S(1)} %collective-permute-done.3.refs_5_), channel_id=1, source_target_pairs={{2,3},{1,0},{6,7},{5,4},{10,11},{9,8},{14,15},{13,12},{18,19},{17,... | collective-permute-start | bytes 786440 | tf_op jit(solution)/shard_map/ppermute | solution.py:254
  31.8 0.1 pad_add_fusion.place
  31.8 0.0 copy-start.1
  31.8 2.2 %load.1.refs_10_ = bf16[32,256,256]{2,1,0:T(8,128)(2,1)S(1)} custom-call(bf16[2,32,256,128]{3,2,1,0:T(8,128)(2,1)} %weights), custom_call_target="tpu_custom_call" | custom-call | bytes 8388608 | tf_op jit(solution)/shard_map/load/pallas_call | solution.py:126
  34.1 0.0 collective-permute-done.1.refs_3_
  34.1 0.0 collective-permute-done.4.refs_6_
  34.1 0.0 collective-permute-done.5.refs_7_
  34.1 1.7 %collective-permute-done.6.refs_8_ = bf16[2,32,16,128]{3,2,1,0:T(8,128)(2,1)S(1)} collective-permute-done((bf16[2,32,16,128]{3,2,1,0:T(8,128)(2,1)S(1)}, bf16[2,32,16,128]{3,2,1,0:T(8,128)(2,1)S(1)}, u32[]{:S(2)}, u32[]{:S(2)}) %collective-permute-start.6) | collective-permute-done | bytes 262176 | tf_op jit(solution)/shard_map/ppermute | solution.py:254
  35.8 5.6 %collective-permute-done.7.refs_9_ = bf16[2,32,16,128]{3,2,1,0:T(8,128)(2,1)S(1)} collective-permute-done((bf16[2,32,16,128]{3,2,1,0:T(8,128)(2,1)S(1)}, bf16[2,32,16,128]{3,2,1,0:T(8,128)(2,1)S(1)}, u32[]{:S(2)}, u32[]{:S(2)}) %collective-permute-start.7) | collective-permute-done | bytes 262176 | tf_op jit(solution)/shard_map/ppermute | solution.py:254
  41.4 0.0 copy-done.1
  41.4 1.8 %beams.1 = (f32[16,2,64,128]{3,2,1,0:T(8,128)S(1)}, bf16[16,2,64,128]{3,2,1,0:T(8,128)(2,1)S(1)}) custom-call(s32[2]{0:T(128)S(1)} %pad_add_fusion.place, bf16[2,32,16,128]{3,2,1,0:T(8,128)(2,1)S(1)} %bitcast.9, bf16[2,32,16,128]{3,2,1,0:T(8,128)(2,1)S(1)} %bitcast.13, bf16[2,32,16,128]{3,2,1,0:T(8,128)(2,1)S(1)} %collective-permute-done.refs_2_, ...), custom_call_target="tpu_custom_call" | custom-call | tf_op jit(solution)/shard_map/beams/pallas_call | solution.py:177
  43.3 2.4 %collective-permute-start.8 = (bf16[16,2,64,128]{3,2,1,0:T(8,128)(2,1)S(1)}, bf16[16,2,64,128]{3,2,1,0:T(8,128)(2,1)S(1)}, u32[]{:S(2)}, u32[]{:S(2)}) collective-permute-start(bf16[16,2,64,128]{3,2,1,0:T(8,128)(2,1)S(1)} %get-tuple-element.14), channel_id=1, source_target_pairs={{0,4},{4,0},{1,5},{5,1},{2,6},{6,2},{3,7},{7,3},{8,12},{12,8},{9,1... | collective-permute-start | bytes 1572872 | tf_op jit(solution)/shard_map/ppermute | solution.py:266
  45.7 1.5 %collective-permute-done.8 = bf16[16,2,64,128]{3,2,1,0:T(8,128)(2,1)S(1)} collective-permute-done((bf16[16,2,64,128]{3,2,1,0:T(8,128)(2,1)S(1)}, bf16[16,2,64,128]{3,2,1,0:T(8,128)(2,1)S(1)}, u32[]{:S(2)}, u32[]{:S(2)}) %collective-permute-start.8) | collective-permute-done | bytes 524320 | tf_op jit(solution)/shard_map/ppermute | solution.py:266
  47.2 0.2 add_convert_fusion
  47.4 17.3 %all_to_all.10 = bf16[16,2,64,128]{3,2,1,0:T(8,128)(2,1)S(1)} all-to-all(bf16[16,2,64,128]{3,2,1,0:T(8,128)(2,1)S(1)} %add_convert_fusion), channel_id=1, replica_groups=mesh['y'=4,'zh'=2,'x'=4,'core'=2,'q'=4] {'y','x'}, dimensions={0} | all-to-all | bytes 1048576 | tf_op jit(solution)/shard_map/all_to_all | solution.py:268
  64.7 0.1 reduce_sum.12
  64.8 13.9 %all_to_all.11 = bf16[8,64,128]{2,1,0:T(8,128)(2,1)S(1)} all-to-all(bf16[8,64,128]{2,1,0:T(8,128)(2,1)S(1)} %bitcast.16), channel_id=1, replica_groups=mesh['y'=4,'zh'=2,'x'=4,'core'=2,'q'=4] {'q','zh'}, dimensions={0} | all-to-all | bytes 262144 | tf_op jit(solution)/shard_map/all_to_all | solution.py:272
  78.7 3.3 %collective-permute-start.9 = (bf16[4,2,64,128]{3,2,1,0:T(8,128)(2,1)S(1)}, bf16[4,2,64,128]{3,2,1,0:T(8,128)(2,1)S(1)}, u32[]{:S(2)}, u32[]{:S(2)}) collective-permute-start(bf16[4,2,64,128]{3,2,1,0:T(8,128)(2,1)S(1)} %bitcast.14), channel_id=1, source_target_pairs={{0,4},{4,0},{1,5},{5,1},{2,6},{6,2},{3,7},{7,3},{8,12},{12,8},{9,1... | collective-permute-start | bytes 393224 | tf_op jit(solution)/shard_map/ppermute | solution.py:274
  82.0 1.0 %collective-permute-done.9.other = bf16[4,2,64,128]{3,2,1,0:T(8,128)(2,1)S(1)} collective-permute-done((bf16[4,2,64,128]{3,2,1,0:T(8,128)(2,1)S(1)}, bf16[4,2,64,128]{3,2,1,0:T(8,128)(2,1)S(1)}, u32[]{:S(2)}, u32[]{:S(2)}) %collective-permute-start.9) | collective-permute-done | bytes 131104 | tf_op jit(solution)/shard_map/ppermute | solution.py:274
  83.0 1.7 %gram.1 = f32[2,1,128,256]{3,2,1,0:T(8,128)} custom-call(s32[2]{0:T(128)S(1)} %pad_add_fusion.place, bf16[4,2,64,128]{3,2,1,0:T(8,128)(2,1)S(1)} %bitcast.15, bf16[4,2,64,128]{3,2,1,0:T(8,128)(2,1)S(1)} %collective-permute-done.9.other), custom_call_target="tpu_custom_call" | custom-call | tf_op jit(solution)/shard_map/gram/pallas_call | solution.py:233
  (1 shorter events, 0.0 us)
Async XLA Ops:
  4.1 15.1 %copy-start = (bf16[64,16,128]{2,1,0:T(8,128)(2,1)S(1)}, bf16[64,16,128]{2,1,0:T(8,128)(2,1)}, u32[]{:S(2)}) copy-start(bf16[64,16,128]{2,1,0:T(8,128)(2,1)} %spectra.2) | copy-start | bytes 786436
  4.1 15.1 %collective-permute-start.2 = (bf16[2,32,16,128]{3,2,1,0:T(8,128)(2,1)}, bf16[2,32,16,128]{3,2,1,0:T(8,128)(2,1)S(1)}, u32[]{:S(2)}, u32[]{:S(2)}) collective-permute-start(bf16[2,32,16,128]{3,2,1,0:T(8,128)(2,1)} %bitcast.6), channel_id=1, source_target_pairs={{0,2},{2,0},{1,3},{3,1},{4,6},{6,4},{5,7},{7,5},{8,10},{10,8},{9,1... | collective-permute-start | bytes 786440 | tf_op jit(solution)/shard_map/ppermute | solution.py:254
  8.0 12.6 %collective-permute-start = (bf16[2,32,16,128]{3,2,1,0:T(8,128)(2,1)}, bf16[2,32,16,128]{3,2,1,0:T(8,128)(2,1)S(1)}, u32[]{:S(2)}, u32[]{:S(2)}) collective-permute-start(bf16[2,32,16,128]{3,2,1,0:T(8,128)(2,1)} %bitcast.7), channel_id=1, source_target_pairs={{0,1},{1,0},{2,3},{3,2},{4,5},{5,4},{6,7},{7,6},{8,9},{9,8},{10,11... | collective-permute-start | bytes 786440 | tf_op jit(solution)/shard_map/ppermute | solution.py:254
  13.7 16.7 %collective-permute-start.3 = (bf16[2,32,16,128]{3,2,1,0:T(8,128)(2,1)}, bf16[2,32,16,128]{3,2,1,0:T(8,128)(2,1)S(1)}, u32[]{:S(2)}, u32[]{:S(2)}) collective-permute-start(bf16[2,32,16,128]{3,2,1,0:T(8,128)(2,1)} %bitcast.10), channel_id=1, source_target_pairs={{0,2},{2,0},{1,3},{3,1},{4,6},{6,4},{5,7},{7,5},{8,10},{10,8},{9,1... | collective-permute-start | bytes 786440 | tf_op jit(solution)/shard_map/ppermute | solution.py:254
  13.9 20.2 %collective-permute-start.1 = (bf16[2,32,16,128]{3,2,1,0:T(8,128)(2,1)}, bf16[2,32,16,128]{3,2,1,0:T(8,128)(2,1)S(1)}, u32[]{:S(2)}, u32[]{:S(2)}) collective-permute-start(bf16[2,32,16,128]{3,2,1,0:T(8,128)(2,1)} %bitcast.11), channel_id=1, source_target_pairs={{0,1},{1,0},{2,3},{3,2},{4,5},{5,4},{6,7},{7,6},{8,9},{9,8},{10,11... | collective-permute-start | bytes 786440 | tf_op jit(solution)/shard_map/ppermute | solution.py:254
  19.2 14.9 %collective-permute-start.4 = (bf16[2,32,16,128]{3,2,1,0:T(8,128)(2,1)S(1)}, bf16[2,32,16,128]{3,2,1,0:T(8,128)(2,1)S(1)}, u32[]{:S(2)}, u32[]{:S(2)}) collective-permute-start(bf16[2,32,16,128]{3,2,1,0:T(8,128)(2,1)S(1)} %bitcast.8), channel_id=1, source_target_pairs={{1,2},{2,1},{5,6},{6,5},{9,10},{10,9},{13,14},{14,13},{17,18},{18,... | collective-permute-start | bytes 786440 | tf_op jit(solution)/shard_map/ppermute | solution.py:254
  19.9 14.3 %collective-permute-start.5 = (bf16[2,32,16,128]{3,2,1,0:T(8,128)(2,1)}, bf16[2,32,16,128]{3,2,1,0:T(8,128)(2,1)S(1)}, u32[]{:S(2)}, u32[]{:S(2)}) collective-permute-start(bf16[2,32,16,128]{3,2,1,0:T(8,128)(2,1)} %bitcast.12), channel_id=1, source_target_pairs={{1,2},{2,1},{5,6},{6,5},{9,10},{10,9},{13,14},{14,13},{17,18},{18,... | collective-permute-start | bytes 786440 | tf_op jit(solution)/shard_map/ppermute | solution.py:254
  20.6 15.3 %collective-permute-start.6 = (bf16[2,32,16,128]{3,2,1,0:T(8,128)(2,1)S(1)}, bf16[2,32,16,128]{3,2,1,0:T(8,128)(2,1)S(1)}, u32[]{:S(2)}, u32[]{:S(2)}) collective-permute-start(bf16[2,32,16,128]{3,2,1,0:T(8,128)(2,1)S(1)} %collective-permute-done.2.refs_4_), channel_id=1, source_target_pairs={{2,3},{1,0},{6,7},{5,4},{10,11},{9,8},{14,15},{13,12},{18,19},{17,... | collective-permute-start | bytes 786440 | tf_op jit(solution)/shard_map/ppermute | solution.py:254
  30.5 11.0 %collective-permute-start.7 = (bf16[2,32,16,128]{3,2,1,0:T(8,128)(2,1)S(1)}, bf16[2,32,16,128]{3,2,1,0:T(8,128)(2,1)S(1)}, u32[]{:S(2)}, u32[]{:S(2)}) collective-permute-start(bf16[2,32,16,128]{3,2,1,0:T(8,128)(2,1)S(1)} %collective-permute-done.3.refs_5_), channel_id=1, source_target_pairs={{2,3},{1,0},{6,7},{5,4},{10,11},{9,8},{14,15},{13,12},{18,19},{17,... | collective-permute-start | bytes 786440 | tf_op jit(solution)/shard_map/ppermute | solution.py:254
  31.8 9.6 %copy-start.1 = (bf16[64,16,128]{2,1,0:T(8,128)(2,1)S(1)}, bf16[64,16,128]{2,1,0:T(8,128)(2,1)}, u32[]{:S(2)}) copy-start(bf16[64,16,128]{2,1,0:T(8,128)(2,1)} %spectra.3) | copy-start | bytes 786436
  43.3 3.9 %collective-permute-start.8 = (bf16[16,2,64,128]{3,2,1,0:T(8,128)(2,1)S(1)}, bf16[16,2,64,128]{3,2,1,0:T(8,128)(2,1)S(1)}, u32[]{:S(2)}, u32[]{:S(2)}) collective-permute-start(bf16[16,2,64,128]{3,2,1,0:T(8,128)(2,1)S(1)} %get-tuple-element.14), channel_id=1, source_target_pairs={{0,4},{4,0},{1,5},{5,1},{2,6},{6,2},{3,7},{7,3},{8,12},{12,8},{9,1... | collective-permute-start | bytes 1572872 | tf_op jit(solution)/shard_map/ppermute | solution.py:266
  78.7 4.3 %collective-permute-start.9 = (bf16[4,2,64,128]{3,2,1,0:T(8,128)(2,1)S(1)}, bf16[4,2,64,128]{3,2,1,0:T(8,128)(2,1)S(1)}, u32[]{:S(2)}, u32[]{:S(2)}) collective-permute-start(bf16[4,2,64,128]{3,2,1,0:T(8,128)(2,1)S(1)} %bitcast.14), channel_id=1, source_target_pairs={{0,4},{4,0},{1,5},{5,1},{2,6},{6,2},{3,7},{7,3},{8,12},{12,8},{9,1... | collective-permute-start | bytes 393224 | tf_op jit(solution)/shard_map/ppermute | solution.py:274

commit v4 on v3

--- a/solution.py
+++ b/solution.py
@@ -93,7 +93,7 @@
             pltpu.SemaphoreType.DMA((steps,)),
             pltpu.SemaphoreType.DMA(()),
         ],
-        compiler_params=pltpu.CompilerParams(vmem_limit_bytes=55 * 2**20),
+        compiler_params=pltpu.CompilerParams(vmem_limit_bytes=50 * 2**20),
         cost_estimate=pl.CostEstimate(
             flops=2 * sensors * snaps * ticks * columns,
             bytes_accessed=2 * sensors * snaps * (ticks + columns),
@@ -164,7 +164,7 @@
             send[to] = jnp.where(second, real_y, imag_y).astype(jnp.bfloat16)
             return 0
 
-        lax.fori_loop(0, weights.shape[0], one_channel, 0, unroll=8)
+        lax.fori_loop(0, weights.shape[0], one_channel, 0, unroll=True)
 
     for q in range(4):
         pl.when(place[0] == q)(functools.partial(run, orders[q]))
@@ -247,7 +247,9 @@
 def local(samples, weights, chosen_frequency_bins):
     chans = chosen_frequency_bins.shape[0]
     place = jnp.stack([lax.axis_index("q"), lax.axis_index("core")]).astype(jnp.int32)
-    own = [spectra_of(samples, chosen_frequency_bins, part, 2) for part in range(2)]
+    bins = pltpu.with_memory_space_constraint(chosen_frequency_bins, pltpu.HBM)
+    samples = pltpu.with_memory_space_constraint(samples, pltpu.HBM)
+    own = [spectra_of(samples, bins, part, 2) for part in range(2)]
     own = [x.reshape(2, chans, *x.shape[1:]) for x in own]
 
     def pass_on(pieces, pairs):

time: 84.9 us -> 83.5 us (0.984)
  Pallas kernels: 13.9 us -> 12 us
    pallas_call x2, Pallas kernels: 8.17 us -> 6.76 us  [spectra_of(): pl.pallas_call(functools.partial(spectra_kernel, part, steps), out_shape=...]
where the time goes in v4:
time: 83.5 us; the launch traced here: 83.3 us
  blocking collectives  31.2 us (37%)
  waiting for transfers between devices  24.2 us (29%)
  starting transfers between devices  15.4 us (18%)
  Pallas kernels  12 us (14%)
    ppermute x8, waiting for transfers between devices, pass_on(): return [lax.ppermute(x, 'q', pairs) for x in pieces]  21.7 us
    all_to_all x1, blocking collectives, local(): mine = lax.all_to_all(mine, ('y', 'x'), 0, 0)  17.3 us
    all_to_all x1, blocking collectives, local(): mine = lax.all_to_all(mine, ('q', 'zh'), 0, 0)  14 us
    ppermute x8, starting transfers between devices, pass_on(): return [lax.ppermute(x, 'q', pairs) for x in pieces]  9.67 us
    pallas_call x2, Pallas kernels, spectra_of(): pl.pallas_call(functools.partial(spectra_kernel, part, steps), out_shape=...  6.76 us
    ppermute x1, starting transfers between devices, local(): other = lax.ppermute(mine, 'core', SWAP)  3.29 us
    ppermute x1, starting transfers between devices, local(): theirs = lax.ppermute(send, 'core', SWAP)  2.44 us
    pallas_call x1, Pallas kernels, load(): pl.pallas_call(load_kernel, out_shape=jax.ShapeDtypeStruct((chans, sensor...  2.21 us
  transfers between devices with their start and end apart: 10, of which 6 were waited for; matrix products, arithmetic and copies ran while one was open for 0% of the time, Pallas kernels for 7%

profile of v4, /device:TPU:1, one launch (start us, length us, event | category | flops | bytes accessed | tf_op | source)
XLA Modules:
  0.0 83.3 jit_solution(10374230359590661069)
XLA Ops:
  0.0 3.4 %spectra.2 = bf16[64,16,128]{2,1,0:T(8,128)(2,1)S(1)} custom-call(s32[32]{0:T(128)} %bins_in.3, bf16[256,16,1024]{2,1,0:T(8,128)(2,1)} %samples.3), custom_call_target="tpu_custom_call" | custom-call | flops 268435456 | bytes 4456448 | tf_op jit(solution)/shard_map/spectra/pallas_call | solution.py:83
  3.4 3.9 %collective-permute-start.2 = (bf16[2,32,16,128]{3,2,1,0:T(8,128)(2,1)S(1)}, bf16[2,32,16,128]{3,2,1,0:T(8,128)(2,1)S(1)}, u32[]{:S(2)}, u32[]{:S(2)}) collective-permute-start(bf16[2,32,16,128]{3,2,1,0:T(8,128)(2,1)S(1)} %bitcast.6), channel_id=1, source_target_pairs={{0,2},{2,0},{1,3},{3,1},{4,6},{6,4},{5,7},{7,5},{8,10},{10,8},{9,1... | collective-permute-start | bytes 786440 | tf_op jit(solution)/shard_map/ppermute | solution.py:256
  7.3 1.6 %collective-permute-start = (bf16[2,32,16,128]{3,2,1,0:T(8,128)(2,1)S(1)}, bf16[2,32,16,128]{3,2,1,0:T(8,128)(2,1)S(1)}, u32[]{:S(2)}, u32[]{:S(2)}) collective-permute-start(bf16[2,32,16,128]{3,2,1,0:T(8,128)(2,1)S(1)} %bitcast.7), channel_id=1, source_target_pairs={{0,1},{1,0},{2,3},{3,2},{4,5},{5,4},{6,7},{7,6},{8,9},{9,8},{10,11... | collective-permute-start | bytes 786440 | tf_op jit(solution)/shard_map/ppermute | solution.py:256
  8.9 3.4 %spectra.3 = bf16[64,16,128]{2,1,0:T(8,128)(2,1)S(1)} custom-call(s32[32]{0:T(128)} %bins_in.3, bf16[256,16,1024]{2,1,0:T(8,128)(2,1)} %samples.3), custom_call_target="tpu_custom_call" | custom-call | flops 268435456 | bytes 4456448 | tf_op jit(solution)/shard_map/spectra/pallas_call | solution.py:83
  12.3 0.2 collective-permute-start.3
  12.5 0.0 collective-permute-start.1
  12.5 5.8 %collective-permute-done.2.refs_4_ = bf16[2,32,16,128]{3,2,1,0:T(8,128)(2,1)S(1)} collective-permute-done((bf16[2,32,16,128]{3,2,1,0:T(8,128)(2,1)S(1)}, bf16[2,32,16,128]{3,2,1,0:T(8,128)(2,1)S(1)}, u32[]{:S(2)}, u32[]{:S(2)}) %collective-permute-start.2) | collective-permute-done | bytes 262176 | tf_op jit(solution)/shard_map/ppermute | solution.py:256
  18.3 0.7 collective-permute-start.4
  19.0 0.7 collective-permute-start.5
  19.7 0.0 collective-permute-done.refs_2_
  19.7 1.3 %collective-permute-start.6 = (bf16[2,32,16,128]{3,2,1,0:T(8,128)(2,1)S(1)}, bf16[2,32,16,128]{3,2,1,0:T(8,128)(2,1)S(1)}, u32[]{:S(2)}, u32[]{:S(2)}) collective-permute-start(bf16[2,32,16,128]{3,2,1,0:T(8,128)(2,1)S(1)} %collective-permute-done.2.refs_4_), channel_id=1, source_target_pairs={{2,3},{1,0},{6,7},{5,4},{10,11},{9,8},{14,15},{13,12},{18,19},{17,... | collective-permute-start | bytes 786440 | tf_op jit(solution)/shard_map/ppermute | solution.py:256
  21.0 8.6 %collective-permute-done.3.refs_5_ = bf16[2,32,16,128]{3,2,1,0:T(8,128)(2,1)S(1)} collective-permute-done((bf16[2,32,16,128]{3,2,1,0:T(8,128)(2,1)S(1)}, bf16[2,32,16,128]{3,2,1,0:T(8,128)(2,1)S(1)}, u32[]{:S(2)}, u32[]{:S(2)}) %collective-permute-start.3) | collective-permute-done | bytes 262176 | tf_op jit(solution)/shard_map/ppermute | solution.py:256
  29.6 1.3 %collective-permute-start.7 = (bf16[2,32,16,128]{3,2,1,0:T(8,128)(2,1)S(1)}, bf16[2,32,16,128]{3,2,1,0:T(8,128)(2,1)S(1)}, u32[]{:S(2)}, u32[]{:S(2)}) collective-permute-start(bf16[2,32,16,128]{3,2,1,0:T(8,128)(2,1)S(1)} %collective-permute-done.3.refs_5_), channel_id=1, source_target_pairs={{2,3},{1,0},{6,7},{5,4},{10,11},{9,8},{14,15},{13,12},{18,19},{17,... | collective-permute-start | bytes 786440 | tf_op jit(solution)/shard_map/ppermute | solution.py:256
  30.9 0.1 pad_add_fusion.place
  30.9 2.2 %load.1.refs_10_ = bf16[32,256,256]{2,1,0:T(8,128)(2,1)S(1)} custom-call(bf16[2,32,256,128]{3,2,1,0:T(8,128)(2,1)} %weights), custom_call_target="tpu_custom_call" | custom-call | bytes 8388608 | tf_op jit(solution)/shard_map/load/pallas_call | solution.py:126
  33.2 0.0 collective-permute-done.1.refs_3_
  33.2 0.0 collective-permute-done.4.refs_6_
  33.2 0.0 collective-permute-done.5.refs_7_
  33.2 1.7 %collective-permute-done.6.refs_8_ = bf16[2,32,16,128]{3,2,1,0:T(8,128)(2,1)S(1)} collective-permute-done((bf16[2,32,16,128]{3,2,1,0:T(8,128)(2,1)S(1)}, bf16[2,32,16,128]{3,2,1,0:T(8,128)(2,1)S(1)}, u32[]{:S(2)}, u32[]{:S(2)}) %collective-permute-start.6) | collective-permute-done | bytes 262176 | tf_op jit(solution)/shard_map/ppermute | solution.py:256
  34.9 5.6 %collective-permute-done.7.refs_9_ = bf16[2,32,16,128]{3,2,1,0:T(8,128)(2,1)S(1)} collective-permute-done((bf16[2,32,16,128]{3,2,1,0:T(8,128)(2,1)S(1)}, bf16[2,32,16,128]{3,2,1,0:T(8,128)(2,1)S(1)}, u32[]{:S(2)}, u32[]{:S(2)}) %collective-permute-start.7) | collective-permute-done | bytes 262176 | tf_op jit(solution)/shard_map/ppermute | solution.py:256
  40.5 1.3 %beams.1 = (f32[16,2,64,128]{3,2,1,0:T(8,128)S(1)}, bf16[16,2,64,128]{3,2,1,0:T(8,128)(2,1)S(1)}) custom-call(s32[2]{0:T(128)S(1)} %pad_add_fusion.place, bf16[2,32,16,128]{3,2,1,0:T(8,128)(2,1)S(1)} %bitcast.9, bf16[2,32,16,128]{3,2,1,0:T(8,128)(2,1)S(1)} %bitcast.13, bf16[2,32,16,128]{3,2,1,0:T(8,128)(2,1)S(1)} %collective-permute-done.refs_2_, ...), custom_call_target="tpu_custom_call" | custom-call | tf_op jit(solution)/shard_map/beams/pallas_call | solution.py:177
  41.8 2.4 %collective-permute-start.8 = (bf16[16,2,64,128]{3,2,1,0:T(8,128)(2,1)S(1)}, bf16[16,2,64,128]{3,2,1,0:T(8,128)(2,1)S(1)}, u32[]{:S(2)}, u32[]{:S(2)}) collective-permute-start(bf16[16,2,64,128]{3,2,1,0:T(8,128)(2,1)S(1)} %get-tuple-element.14), channel_id=1, source_target_pairs={{0,4},{4,0},{1,5},{5,1},{2,6},{6,2},{3,7},{7,3},{8,12},{12,8},{9,1... | collective-permute-start | bytes 1572872 | tf_op jit(solution)/shard_map/ppermute | solution.py:268
  44.3 1.5 %collective-permute-done.8 = bf16[16,2,64,128]{3,2,1,0:T(8,128)(2,1)S(1)} collective-permute-done((bf16[16,2,64,128]{3,2,1,0:T(8,128)(2,1)S(1)}, bf16[16,2,64,128]{3,2,1,0:T(8,128)(2,1)S(1)}, u32[]{:S(2)}, u32[]{:S(2)}) %collective-permute-start.8) | collective-permute-done | bytes 524320 | tf_op jit(solution)/shard_map/ppermute | solution.py:268
  45.8 0.2 add_convert_fusion
  46.0 17.3 %all_to_all.10 = bf16[16,2,64,128]{3,2,1,0:T(8,128)(2,1)S(1)} all-to-all(bf16[16,2,64,128]{3,2,1,0:T(8,128)(2,1)S(1)} %add_convert_fusion), channel_id=1, replica_groups=mesh['y'=4,'zh'=2,'x'=4,'core'=2,'q'=4] {'y','x'}, dimensions={0} | all-to-all | bytes 1048576 | tf_op jit(solution)/shard_map/all_to_all | solution.py:270
  63.2 0.1 reduce_sum.12
  63.3 14.0 %all_to_all.11 = bf16[8,64,128]{2,1,0:T(8,128)(2,1)S(1)} all-to-all(bf16[8,64,128]{2,1,0:T(8,128)(2,1)S(1)} %bitcast.16), channel_id=1, replica_groups=mesh['y'=4,'zh'=2,'x'=4,'core'=2,'q'=4] {'q','zh'}, dimensions={0} | all-to-all | bytes 262144 | tf_op jit(solution)/shard_map/all_to_all | solution.py:274
  77.3 3.3 %collective-permute-start.9 = (bf16[4,2,64,128]{3,2,1,0:T(8,128)(2,1)S(1)}, bf16[4,2,64,128]{3,2,1,0:T(8,128)(2,1)S(1)}, u32[]{:S(2)}, u32[]{:S(2)}) collective-permute-start(bf16[4,2,64,128]{3,2,1,0:T(8,128)(2,1)S(1)} %bitcast.14), channel_id=1, source_target_pairs={{0,4},{4,0},{1,5},{5,1},{2,6},{6,2},{3,7},{7,3},{8,12},{12,8},{9,1... | collective-permute-start | bytes 393224 | tf_op jit(solution)/shard_map/ppermute | solution.py:276
  80.6 1.0 %collective-permute-done.9.other = bf16[4,2,64,128]{3,2,1,0:T(8,128)(2,1)S(1)} collective-permute-done((bf16[4,2,64,128]{3,2,1,0:T(8,128)(2,1)S(1)}, bf16[4,2,64,128]{3,2,1,0:T(8,128)(2,1)S(1)}, u32[]{:S(2)}, u32[]{:S(2)}) %collective-permute-start.9) | collective-permute-done | bytes 131104 | tf_op jit(solution)/shard_map/ppermute | solution.py:276
  81.6 1.7 %gram.1 = f32[2,1,128,256]{3,2,1,0:T(8,128)} custom-call(s32[2]{0:T(128)S(1)} %pad_add_fusion.place, bf16[4,2,64,128]{3,2,1,0:T(8,128)(2,1)S(1)} %bitcast.15, bf16[4,2,64,128]{3,2,1,0:T(8,128)(2,1)S(1)} %collective-permute-done.9.other), custom_call_target="tpu_custom_call" | custom-call | tf_op jit(solution)/shard_map/gram/pallas_call | solution.py:233
  (1 shorter events, 0.0 us)
Async XLA Ops:
  3.4 14.9 %collective-permute-start.2 = (bf16[2,32,16,128]{3,2,1,0:T(8,128)(2,1)S(1)}, bf16[2,32,16,128]{3,2,1,0:T(8,128)(2,1)S(1)}, u32[]{:S(2)}, u32[]{:S(2)}) collective-permute-start(bf16[2,32,16,128]{3,2,1,0:T(8,128)(2,1)S(1)} %bitcast.6), channel_id=1, source_target_pairs={{0,2},{2,0},{1,3},{3,1},{4,6},{6,4},{5,7},{7,5},{8,10},{10,8},{9,1... | collective-permute-start | bytes 786440 | tf_op jit(solution)/shard_map/ppermute | solution.py:256
  7.3 12.4 %collective-permute-start = (bf16[2,32,16,128]{3,2,1,0:T(8,128)(2,1)S(1)}, bf16[2,32,16,128]{3,2,1,0:T(8,128)(2,1)S(1)}, u32[]{:S(2)}, u32[]{:S(2)}) collective-permute-start(bf16[2,32,16,128]{3,2,1,0:T(8,128)(2,1)S(1)} %bitcast.7), channel_id=1, source_target_pairs={{0,1},{1,0},{2,3},{3,2},{4,5},{5,4},{6,7},{7,6},{8,9},{9,8},{10,11... | collective-permute-start | bytes 786440 | tf_op jit(solution)/shard_map/ppermute | solution.py:256
  12.3 17.2 %collective-permute-start.3 = (bf16[2,32,16,128]{3,2,1,0:T(8,128)(2,1)S(1)}, bf16[2,32,16,128]{3,2,1,0:T(8,128)(2,1)S(1)}, u32[]{:S(2)}, u32[]{:S(2)}) collective-permute-start(bf16[2,32,16,128]{3,2,1,0:T(8,128)(2,1)S(1)} %bitcast.10), channel_id=1, source_target_pairs={{0,2},{2,0},{1,3},{3,1},{4,6},{6,4},{5,7},{7,5},{8,10},{10,8},{9,1... | collective-permute-start | bytes 786440 | tf_op jit(solution)/shard_map/ppermute | solution.py:256
  12.5 20.7 %collective-permute-start.1 = (bf16[2,32,16,128]{3,2,1,0:T(8,128)(2,1)S(1)}, bf16[2,32,16,128]{3,2,1,0:T(8,128)(2,1)S(1)}, u32[]{:S(2)}, u32[]{:S(2)}) collective-permute-start(bf16[2,32,16,128]{3,2,1,0:T(8,128)(2,1)S(1)} %bitcast.11), channel_id=1, source_target_pairs={{0,1},{1,0},{2,3},{3,2},{4,5},{5,4},{6,7},{7,6},{8,9},{9,8},{10,11... | collective-permute-start | bytes 786440 | tf_op jit(solution)/shard_map/ppermute | solution.py:256
  18.3 14.9 %collective-permute-start.4 = (bf16[2,32,16,128]{3,2,1,0:T(8,128)(2,1)S(1)}, bf16[2,32,16,128]{3,2,1,0:T(8,128)(2,1)S(1)}, u32[]{:S(2)}, u32[]{:S(2)}) collective-permute-start(bf16[2,32,16,128]{3,2,1,0:T(8,128)(2,1)S(1)} %bitcast.8), channel_id=1, source_target_pairs={{1,2},{2,1},{5,6},{6,5},{9,10},{10,9},{13,14},{14,13},{17,18},{18,... | collective-permute-start | bytes 786440 | tf_op jit(solution)/shard_map/ppermute | solution.py:256
  19.0 14.2 %collective-permute-start.5 = (bf16[2,32,16,128]{3,2,1,0:T(8,128)(2,1)S(1)}, bf16[2,32,16,128]{3,2,1,0:T(8,128)(2,1)S(1)}, u32[]{:S(2)}, u32[]{:S(2)}) collective-permute-start(bf16[2,32,16,128]{3,2,1,0:T(8,128)(2,1)S(1)} %bitcast.12), channel_id=1, source_target_pairs={{1,2},{2,1},{5,6},{6,5},{9,10},{10,9},{13,14},{14,13},{17,18},{18,... | collective-permute-start | bytes 786440 | tf_op jit(solution)/shard_map/ppermute | solution.py:256
  19.7 15.2 %collective-permute-start.6 = (bf16[2,32,16,128]{3,2,1,0:T(8,128)(2,1)S(1)}, bf16[2,32,16,128]{3,2,1,0:T(8,128)(2,1)S(1)}, u32[]{:S(2)}, u32[]{:S(2)}) collective-permute-start(bf16[2,32,16,128]{3,2,1,0:T(8,128)(2,1)S(1)} %collective-permute-done.2.refs_4_), channel_id=1, source_target_pairs={{2,3},{1,0},{6,7},{5,4},{10,11},{9,8},{14,15},{13,12},{18,19},{17,... | collective-permute-start | bytes 786440 | tf_op jit(solution)/shard_map/ppermute | solution.py:256
  29.6 10.9 %collective-permute-start.7 = (bf16[2,32,16,128]{3,2,1,0:T(8,128)(2,1)S(1)}, bf16[2,32,16,128]{3,2,1,0:T(8,128)(2,1)S(1)}, u32[]{:S(2)}, u32[]{:S(2)}) collective-permute-start(bf16[2,32,16,128]{3,2,1,0:T(8,128)(2,1)S(1)} %collective-permute-done.3.refs_5_), channel_id=1, source_target_pairs={{2,3},{1,0},{6,7},{5,4},{10,11},{9,8},{14,15},{13,12},{18,19},{17,... | collective-permute-start | bytes 786440 | tf_op jit(solution)/shard_map/ppermute | solution.py:256
  41.8 4.0 %collective-permute-start.8 = (bf16[16,2,64,128]{3,2,1,0:T(8,128)(2,1)S(1)}, bf16[16,2,64,128]{3,2,1,0:T(8,128)(2,1)S(1)}, u32[]{:S(2)}, u32[]{:S(2)}) collective-permute-start(bf16[16,2,64,128]{3,2,1,0:T(8,128)(2,1)S(1)} %get-tuple-element.14), channel_id=1, source_target_pairs={{0,4},{4,0},{1,5},{5,1},{2,6},{6,2},{3,7},{7,3},{8,12},{12,8},{9,1... | collective-permute-start | bytes 1572872 | tf_op jit(solution)/shard_map/ppermute | solution.py:268
  77.3 4.3 %collective-permute-start.9 = (bf16[4,2,64,128]{3,2,1,0:T(8,128)(2,1)S(1)}, bf16[4,2,64,128]{3,2,1,0:T(8,128)(2,1)S(1)}, u32[]{:S(2)}, u32[]{:S(2)}) collective-permute-start(bf16[4,2,64,128]{3,2,1,0:T(8,128)(2,1)S(1)} %bitcast.14), channel_id=1, source_target_pairs={{0,4},{4,0},{1,5},{5,1},{2,6},{6,2},{3,7},{7,3},{8,12},{12,8},{9,1... | collective-permute-start | bytes 393224 | tf_op jit(solution)/shard_map/ppermute | solution.py:276

commit v5 on v4

--- a/solution.py
+++ b/solution.py
@@ -137,10 +137,11 @@
     )(weights)
 
 
-def beams_kernel(place, *refs):
+def beams_kernel(*refs):
     weights, keep, send = refs[-3:]
     own, near, far, middle, out = [refs[2 * k : 2 * k + 2] for k in range(5)]
-    second = place[1] == 1
+    q_here = lax.axis_index("q")
+    second = lax.axis_index("core") == 1
     orders = (
         (own, near, far, out),
         (near, own, middle, far),
@@ -167,10 +168,10 @@
         lax.fori_loop(0, weights.shape[0], one_channel, 0, unroll=True)
 
     for q in range(4):
-        pl.when(place[0] == q)(functools.partial(run, orders[q]))
-
-
-def partial_beams(place, blocks, weights):
+        pl.when(q_here == q)(functools.partial(run, orders[q]))
+
+
+def partial_beams(blocks, weights):
     _, chans, snaps, sensors = blocks[0].shape
     beams = weights.shape[2] // 2
     shape = (chans // 2, 2, 4 * snaps, beams)
@@ -180,16 +181,15 @@
             jax.ShapeDtypeStruct(shape, jnp.float32),
             jax.ShapeDtypeStruct(shape, jnp.bfloat16),
         ],
-        in_specs=[pl.BlockSpec(memory_space=pltpu.SMEM)]
-        + [pl.BlockSpec(memory_space=pltpu.VMEM)] * (len(blocks) + 1),
+        in_specs=[pl.BlockSpec(memory_space=pltpu.VMEM)] * (len(blocks) + 1),
         out_specs=[pl.BlockSpec(memory_space=pltpu.VMEM)] * 2,
         compiler_params=pltpu.CompilerParams(vmem_limit_bytes=32 * 2**20),
         name="beams",
-    )(place, *blocks, weights)
-
-
-def gram_kernel(place, mine, other, out):
-    q, core = place[0], place[1]
+    )(*blocks, weights)
+
+
+def gram_kernel(mine, other, out):
+    q, core = lax.axis_index("q"), lax.axis_index("core")
     snaps = mine.shape[2]
     whole = []
     for part in range(2):
@@ -228,25 +228,20 @@
     out[1, 0] = contract(jnp.concatenate([left_imag, -left_real], axis=0)) * inverse
 
 
-def gram(place, mine, other):
+def gram(mine, other):
     beams = mine.shape[3]
     return pl.pallas_call(
         gram_kernel,
         out_shape=jax.ShapeDtypeStruct((2, 1, beams, 2 * beams), jnp.float32),
-        in_specs=[
-            pl.BlockSpec(memory_space=pltpu.SMEM),
-            pl.BlockSpec(memory_space=pltpu.VMEM),
-            pl.BlockSpec(memory_space=pltpu.VMEM),
-        ],
+        in_specs=[pl.BlockSpec(memory_space=pltpu.VMEM)] * 2,
         out_specs=pl.BlockSpec(memory_space=pltpu.VMEM),
         compiler_params=pltpu.CompilerParams(vmem_limit_bytes=32 * 2**20),
         name="gram",
-    )(place, mine, other)
+    )(mine, other)
 
 
 def local(samples, weights, chosen_frequency_bins):
     chans = chosen_frequency_bins.shape[0]
-    place = jnp.stack([lax.axis_index("q"), lax.axis_index("core")]).astype(jnp.int32)
     bins = pltpu.with_memory_space_constraint(chosen_frequency_bins, pltpu.HBM)
     samples = pltpu.with_memory_space_constraint(samples, pltpu.HBM)
     own = [spectra_of(samples, bins, part, 2) for part in range(2)]
@@ -264,7 +259,7 @@
     middle = pass_on([after(x, far[0]) for x in own], MIDDLE)
     weights = load(after(weights, far[-1]))
     blocks = own + near + far + middle + out
-    keep, send = partial_beams(place, blocks, weights)
+    keep, send = partial_beams(blocks, weights)
     theirs = lax.ppermute(send, "core", SWAP)
     mine = (keep + theirs.astype(jnp.float32)).astype(jnp.bfloat16)
     mine = lax.all_to_all(mine, ("y", "x"), 0, 0)
@@ -274,7 +269,7 @@
     mine = lax.all_to_all(mine, ("q", "zh"), 0, 0)
     mine = mine.reshape(4, 2, *mine.shape[1:])
     other = lax.ppermute(mine, "core", SWAP)
-    return gram(place, mine, other)
+    return gram(mine, other)
 
 
 def solution(mesh):

time: 83.5 us -> 82.4 us (0.987)
  Pallas kernels: 12 us -> 10.9 us
where the time goes in v5:
time: 82.4 us; the launch traced here: 82.2 us
  blocking collectives  31.2 us (38%)
  waiting for transfers between devices  24.3 us (29%)
  starting transfers between devices  15.4 us (19%)
  Pallas kernels  10.9 us (13%)
    ppermute x8, waiting for transfers between devices, pass_on(): return [lax.ppermute(x, 'q', pairs) for x in pieces]  21.7 us
    all_to_all x1, blocking collectives, local(): mine = lax.all_to_all(mine, ('y', 'x'), 0, 0)  17.3 us
    all_to_all x1, blocking collectives, local(): mine = lax.all_to_all(mine, ('q', 'zh'), 0, 0)  14 us
    ppermute x8, starting transfers between devices, pass_on(): return [lax.ppermute(x, 'q', pairs) for x in pieces]  9.68 us
    pallas_call x2, Pallas kernels, spectra_of(): pl.pallas_call(functools.partial(spectra_kernel, part, steps), out_shape=...  6.75 us
    ppermute x1, starting transfers between devices, local(): other = lax.ppermute(mine, 'core', SWAP)  3.29 us
    ppermute x1, starting transfers between devices, local(): theirs = lax.ppermute(send, 'core', SWAP)  2.44 us
    pallas_call x1, Pallas kernels, load(): pl.pallas_call(load_kernel, out_shape=jax.ShapeDtypeStruct((chans, sensor...  2.21 us
  transfers between devices with their start and end apart: 10, of which 6 were waited for; matrix products, arithmetic and copies ran while one was open for 0% of the time, Pallas kernels for 7%

profile of v5, /device:TPU:1, one launch (start us, length us, event | category | flops | bytes accessed | tf_op | source)
XLA Modules:
  0.0 82.2 jit_solution(961930869374584079)
XLA Ops:
  0.0 3.4 %spectra.2 = bf16[64,16,128]{2,1,0:T(8,128)(2,1)S(1)} custom-call(s32[32]{0:T(128)} %bins_in.3, bf16[256,16,1024]{2,1,0:T(8,128)(2,1)} %samples.3), custom_call_target="tpu_custom_call" | custom-call | flops 268435456 | bytes 4456448 | tf_op jit(solution)/shard_map/spectra/pallas_call | solution.py:83
  3.4 3.9 %collective-permute-start.2 = (bf16[2,32,16,128]{3,2,1,0:T(8,128)(2,1)S(1)}, bf16[2,32,16,128]{3,2,1,0:T(8,128)(2,1)S(1)}, u32[]{:S(2)}, u32[]{:S(2)}) collective-permute-start(bf16[2,32,16,128]{3,2,1,0:T(8,128)(2,1)S(1)} %bitcast.4), channel_id=1, source_target_pairs={{0,2},{2,0},{1,3},{3,1},{4,6},{6,4},{5,7},{7,5},{8,10},{10,8},{9,1... | collective-permute-start | bytes 786440 | tf_op jit(solution)/shard_map/ppermute | solution.py:251
  7.3 1.6 %collective-permute-start = (bf16[2,32,16,128]{3,2,1,0:T(8,128)(2,1)S(1)}, bf16[2,32,16,128]{3,2,1,0:T(8,128)(2,1)S(1)}, u32[]{:S(2)}, u32[]{:S(2)}) collective-permute-start(bf16[2,32,16,128]{3,2,1,0:T(8,128)(2,1)S(1)} %bitcast.5), channel_id=1, source_target_pairs={{0,1},{1,0},{2,3},{3,2},{4,5},{5,4},{6,7},{7,6},{8,9},{9,8},{10,11... | collective-permute-start | bytes 786440 | tf_op jit(solution)/shard_map/ppermute | solution.py:251
  8.9 3.4 %spectra.3 = bf16[64,16,128]{2,1,0:T(8,128)(2,1)S(1)} custom-call(s32[32]{0:T(128)} %bins_in.3, bf16[256,16,1024]{2,1,0:T(8,128)(2,1)} %samples.3), custom_call_target="tpu_custom_call" | custom-call | flops 268435456 | bytes 4456448 | tf_op jit(solution)/shard_map/spectra/pallas_call | solution.py:83
  12.3 0.2 collective-permute-start.3
  12.5 0.0 collective-permute-start.1
  12.5 5.8 %collective-permute-done.2.refs_4_ = bf16[2,32,16,128]{3,2,1,0:T(8,128)(2,1)S(1)} collective-permute-done((bf16[2,32,16,128]{3,2,1,0:T(8,128)(2,1)S(1)}, bf16[2,32,16,128]{3,2,1,0:T(8,128)(2,1)S(1)}, u32[]{:S(2)}, u32[]{:S(2)}) %collective-permute-start.2) | collective-permute-done | bytes 262176 | tf_op jit(solution)/shard_map/ppermute | solution.py:251
  18.3 0.7 collective-permute-start.4
  19.0 0.7 collective-permute-start.5
  19.7 0.0 collective-permute-done.refs_2_
  19.7 1.3 %collective-permute-start.6 = (bf16[2,32,16,128]{3,2,1,0:T(8,128)(2,1)S(1)}, bf16[2,32,16,128]{3,2,1,0:T(8,128)(2,1)S(1)}, u32[]{:S(2)}, u32[]{:S(2)}) collective-permute-start(bf16[2,32,16,128]{3,2,1,0:T(8,128)(2,1)S(1)} %collective-permute-done.2.refs_4_), channel_id=1, source_target_pairs={{2,3},{1,0},{6,7},{5,4},{10,11},{9,8},{14,15},{13,12},{18,19},{17,... | collective-permute-start | bytes 786440 | tf_op jit(solution)/shard_map/ppermute | solution.py:251
  21.0 8.6 %collective-permute-done.3.refs_5_ = bf16[2,32,16,128]{3,2,1,0:T(8,128)(2,1)S(1)} collective-permute-done((bf16[2,32,16,128]{3,2,1,0:T(8,128)(2,1)S(1)}, bf16[2,32,16,128]{3,2,1,0:T(8,128)(2,1)S(1)}, u32[]{:S(2)}, u32[]{:S(2)}) %collective-permute-start.3) | collective-permute-done | bytes 262176 | tf_op jit(solution)/shard_map/ppermute | solution.py:251
  29.6 1.3 %collective-permute-start.7 = (bf16[2,32,16,128]{3,2,1,0:T(8,128)(2,1)S(1)}, bf16[2,32,16,128]{3,2,1,0:T(8,128)(2,1)S(1)}, u32[]{:S(2)}, u32[]{:S(2)}) collective-permute-start(bf16[2,32,16,128]{3,2,1,0:T(8,128)(2,1)S(1)} %collective-permute-done.3.refs_5_), channel_id=1, source_target_pairs={{2,3},{1,0},{6,7},{5,4},{10,11},{9,8},{14,15},{13,12},{18,19},{17,... | collective-permute-start | bytes 786440 | tf_op jit(solution)/shard_map/ppermute | solution.py:251
  30.9 2.2 %load.1.refs_10_ = bf16[32,256,256]{2,1,0:T(8,128)(2,1)S(1)} custom-call(bf16[2,32,256,128]{3,2,1,0:T(8,128)(2,1)} %weights), custom_call_target="tpu_custom_call" | custom-call | bytes 8388608 | tf_op jit(solution)/shard_map/load/pallas_call | solution.py:126
  33.1 0.0 collective-permute-done.1.refs_3_
  33.1 0.0 collective-permute-done.4.refs_6_
  33.1 0.0 collective-permute-done.5.refs_7_
  33.1 1.7 %collective-permute-done.6.refs_8_ = bf16[2,32,16,128]{3,2,1,0:T(8,128)(2,1)S(1)} collective-permute-done((bf16[2,32,16,128]{3,2,1,0:T(8,128)(2,1)S(1)}, bf16[2,32,16,128]{3,2,1,0:T(8,128)(2,1)S(1)}, u32[]{:S(2)}, u32[]{:S(2)}) %collective-permute-start.6) | collective-permute-done | bytes 262176 | tf_op jit(solution)/shard_map/ppermute | solution.py:251
  34.9 5.6 %collective-permute-done.7.refs_9_ = bf16[2,32,16,128]{3,2,1,0:T(8,128)(2,1)S(1)} collective-permute-done((bf16[2,32,16,128]{3,2,1,0:T(8,128)(2,1)S(1)}, bf16[2,32,16,128]{3,2,1,0:T(8,128)(2,1)S(1)}, u32[]{:S(2)}, u32[]{:S(2)}) %collective-permute-start.7) | collective-permute-done | bytes 262176 | tf_op jit(solution)/shard_map/ppermute | solution.py:251
  40.5 0.8 beams.1
  41.3 2.4 %collective-permute-start.8 = (bf16[16,2,64,128]{3,2,1,0:T(8,128)(2,1)S(1)}, bf16[16,2,64,128]{3,2,1,0:T(8,128)(2,1)S(1)}, u32[]{:S(2)}, u32[]{:S(2)}) collective-permute-start(bf16[16,2,64,128]{3,2,1,0:T(8,128)(2,1)S(1)} %get-tuple-element.14), channel_id=1, source_target_pairs={{0,4},{4,0},{1,5},{5,1},{2,6},{6,2},{3,7},{7,3},{8,12},{12,8},{9,1... | collective-permute-start | bytes 1572872 | tf_op jit(solution)/shard_map/ppermute | solution.py:263
  43.7 1.5 %collective-permute-done.8 = bf16[16,2,64,128]{3,2,1,0:T(8,128)(2,1)S(1)} collective-permute-done((bf16[16,2,64,128]{3,2,1,0:T(8,128)(2,1)S(1)}, bf16[16,2,64,128]{3,2,1,0:T(8,128)(2,1)S(1)}, u32[]{:S(2)}, u32[]{:S(2)}) %collective-permute-start.8) | collective-permute-done | bytes 524320 | tf_op jit(solution)/shard_map/ppermute | solution.py:263
  45.3 0.1 add_convert_fusion
  45.4 17.3 %all_to_all.10 = bf16[16,2,64,128]{3,2,1,0:T(8,128)(2,1)S(1)} all-to-all(bf16[16,2,64,128]{3,2,1,0:T(8,128)(2,1)S(1)} %add_convert_fusion), channel_id=1, replica_groups=mesh['y'=4,'zh'=2,'x'=4,'core'=2,'q'=4] {'y','x'}, dimensions={0} | all-to-all | bytes 1048576 | tf_op jit(solution)/shard_map/all_to_all | solution.py:265
  62.7 0.1 reduce_sum.12
  62.8 14.0 %all_to_all.11 = bf16[8,64,128]{2,1,0:T(8,128)(2,1)S(1)} all-to-all(bf16[8,64,128]{2,1,0:T(8,128)(2,1)S(1)} %bitcast.14), channel_id=1, replica_groups=mesh['y'=4,'zh'=2,'x'=4,'core'=2,'q'=4] {'q','zh'}, dimensions={0} | all-to-all | bytes 262144 | tf_op jit(solution)/shard_map/all_to_all | solution.py:269
  76.8 3.3 %collective-permute-start.9 = (bf16[4,2,64,128]{3,2,1,0:T(8,128)(2,1)S(1)}, bf16[4,2,64,128]{3,2,1,0:T(8,128)(2,1)S(1)}, u32[]{:S(2)}, u32[]{:S(2)}) collective-permute-start(bf16[4,2,64,128]{3,2,1,0:T(8,128)(2,1)S(1)} %bitcast.12), channel_id=1, source_target_pairs={{0,4},{4,0},{1,5},{5,1},{2,6},{6,2},{3,7},{7,3},{8,12},{12,8},{9,1... | collective-permute-start | bytes 393224 | tf_op jit(solution)/shard_map/ppermute | solution.py:271
  80.0 1.0 %collective-permute-done.9.other = bf16[4,2,64,128]{3,2,1,0:T(8,128)(2,1)S(1)} collective-permute-done((bf16[4,2,64,128]{3,2,1,0:T(8,128)(2,1)S(1)}, bf16[4,2,64,128]{3,2,1,0:T(8,128)(2,1)S(1)}, u32[]{:S(2)}, u32[]{:S(2)}) %collective-permute-start.9) | collective-permute-done | bytes 131104 | tf_op jit(solution)/shard_map/ppermute | solution.py:271
  81.0 1.2 %gram.1 = f32[2,1,128,256]{3,2,1,0:T(8,128)} custom-call(bf16[4,2,64,128]{3,2,1,0:T(8,128)(2,1)S(1)} %bitcast.13, bf16[4,2,64,128]{3,2,1,0:T(8,128)(2,1)S(1)} %collective-permute-done.9.other), custom_call_target="tpu_custom_call" | custom-call | tf_op jit(solution)/shard_map/gram/pallas_call | solution.py:233
  (1 shorter events, 0.0 us)
Async XLA Ops:
  3.4 14.9 %collective-permute-start.2 = (bf16[2,32,16,128]{3,2,1,0:T(8,128)(2,1)S(1)}, bf16[2,32,16,128]{3,2,1,0:T(8,128)(2,1)S(1)}, u32[]{:S(2)}, u32[]{:S(2)}) collective-permute-start(bf16[2,32,16,128]{3,2,1,0:T(8,128)(2,1)S(1)} %bitcast.4), channel_id=1, source_target_pairs={{0,2},{2,0},{1,3},{3,1},{4,6},{6,4},{5,7},{7,5},{8,10},{10,8},{9,1... | collective-permute-start | bytes 786440 | tf_op jit(solution)/shard_map/ppermute | solution.py:251
  7.3 12.4 %collective-permute-start = (bf16[2,32,16,128]{3,2,1,0:T(8,128)(2,1)S(1)}, bf16[2,32,16,128]{3,2,1,0:T(8,128)(2,1)S(1)}, u32[]{:S(2)}, u32[]{:S(2)}) collective-permute-start(bf16[2,32,16,128]{3,2,1,0:T(8,128)(2,1)S(1)} %bitcast.5), channel_id=1, source_target_pairs={{0,1},{1,0},{2,3},{3,2},{4,5},{5,4},{6,7},{7,6},{8,9},{9,8},{10,11... | collective-permute-start | bytes 786440 | tf_op jit(solution)/shard_map/ppermute | solution.py:251
  12.3 17.3 %collective-permute-start.3 = (bf16[2,32,16,128]{3,2,1,0:T(8,128)(2,1)S(1)}, bf16[2,32,16,128]{3,2,1,0:T(8,128)(2,1)S(1)}, u32[]{:S(2)}, u32[]{:S(2)}) collective-permute-start(bf16[2,32,16,128]{3,2,1,0:T(8,128)(2,1)S(1)} %bitcast.8), channel_id=1, source_target_pairs={{0,2},{2,0},{1,3},{3,1},{4,6},{6,4},{5,7},{7,5},{8,10},{10,8},{9,1... | collective-permute-start | bytes 786440 | tf_op jit(solution)/shard_map/ppermute | solution.py:251
  12.5 20.6 %collective-permute-start.1 = (bf16[2,32,16,128]{3,2,1,0:T(8,128)(2,1)S(1)}, bf16[2,32,16,128]{3,2,1,0:T(8,128)(2,1)S(1)}, u32[]{:S(2)}, u32[]{:S(2)}) collective-permute-start(bf16[2,32,16,128]{3,2,1,0:T(8,128)(2,1)S(1)} %bitcast.9), channel_id=1, source_target_pairs={{0,1},{1,0},{2,3},{3,2},{4,5},{5,4},{6,7},{7,6},{8,9},{9,8},{10,11... | collective-permute-start | bytes 786440 | tf_op jit(solution)/shard_map/ppermute | solution.py:251
  18.3 14.8 %collective-permute-start.4 = (bf16[2,32,16,128]{3,2,1,0:T(8,128)(2,1)S(1)}, bf16[2,32,16,128]{3,2,1,0:T(8,128)(2,1)S(1)}, u32[]{:S(2)}, u32[]{:S(2)}) collective-permute-start(bf16[2,32,16,128]{3,2,1,0:T(8,128)(2,1)S(1)} %bitcast.6), channel_id=1, source_target_pairs={{1,2},{2,1},{5,6},{6,5},{9,10},{10,9},{13,14},{14,13},{17,18},{18,... | collective-permute-start | bytes 786440 | tf_op jit(solution)/shard_map/ppermute | solution.py:251
  19.0 14.1 %collective-permute-start.5 = (bf16[2,32,16,128]{3,2,1,0:T(8,128)(2,1)S(1)}, bf16[2,32,16,128]{3,2,1,0:T(8,128)(2,1)S(1)}, u32[]{:S(2)}, u32[]{:S(2)}) collective-permute-start(bf16[2,32,16,128]{3,2,1,0:T(8,128)(2,1)S(1)} %bitcast.10), channel_id=1, source_target_pairs={{1,2},{2,1},{5,6},{6,5},{9,10},{10,9},{13,14},{14,13},{17,18},{18,... | collective-permute-start | bytes 786440 | tf_op jit(solution)/shard_map/ppermute | solution.py:251
  19.7 15.2 %collective-permute-start.6 = (bf16[2,32,16,128]{3,2,1,0:T(8,128)(2,1)S(1)}, bf16[2,32,16,128]{3,2,1,0:T(8,128)(2,1)S(1)}, u32[]{:S(2)}, u32[]{:S(2)}) collective-permute-start(bf16[2,32,16,128]{3,2,1,0:T(8,128)(2,1)S(1)} %collective-permute-done.2.refs_4_), channel_id=1, source_target_pairs={{2,3},{1,0},{6,7},{5,4},{10,11},{9,8},{14,15},{13,12},{18,19},{17,... | collective-permute-start | bytes 786440 | tf_op jit(solution)/shard_map/ppermute | solution.py:251
  29.6 10.9 %collective-permute-start.7 = (bf16[2,32,16,128]{3,2,1,0:T(8,128)(2,1)S(1)}, bf16[2,32,16,128]{3,2,1,0:T(8,128)(2,1)S(1)}, u32[]{:S(2)}, u32[]{:S(2)}) collective-permute-start(bf16[2,32,16,128]{3,2,1,0:T(8,128)(2,1)S(1)} %collective-permute-done.3.refs_5_), channel_id=1, source_target_pairs={{2,3},{1,0},{6,7},{5,4},{10,11},{9,8},{14,15},{13,12},{18,19},{17,... | collective-permute-start | bytes 786440 | tf_op jit(solution)/shard_map/ppermute | solution.py:251
  41.3 4.0 %collective-permute-start.8 = (bf16[16,2,64,128]{3,2,1,0:T(8,128)(2,1)S(1)}, bf16[16,2,64,128]{3,2,1,0:T(8,128)(2,1)S(1)}, u32[]{:S(2)}, u32[]{:S(2)}) collective-permute-start(bf16[16,2,64,128]{3,2,1,0:T(8,128)(2,1)S(1)} %get-tuple-element.14), channel_id=1, source_target_pairs={{0,4},{4,0},{1,5},{5,1},{2,6},{6,2},{3,7},{7,3},{8,12},{12,8},{9,1... | collective-permute-start | bytes 1572872 | tf_op jit(solution)/shard_map/ppermute | solution.py:263
  76.8 4.3 %collective-permute-start.9 = (bf16[4,2,64,128]{3,2,1,0:T(8,128)(2,1)S(1)}, bf16[4,2,64,128]{3,2,1,0:T(8,128)(2,1)S(1)}, u32[]{:S(2)}, u32[]{:S(2)}) collective-permute-start(bf16[4,2,64,128]{3,2,1,0:T(8,128)(2,1)S(1)} %bitcast.12), channel_id=1, source_target_pairs={{0,4},{4,0},{1,5},{5,1},{2,6},{6,2},{3,7},{7,3},{8,12},{12,8},{9,1... | collective-permute-start | bytes 393224 | tf_op jit(solution)/shard_map/ppermute | solution.py:271

commit v6 on v5

--- a/solution.py
+++ b/solution.py
@@ -72,7 +72,7 @@
     for n in range(snaps):
         one = rows[pl.ds(n, sensors, stride=snaps), :].T[:columns]
         turned[pl.ds(n, columns, stride=snaps), :] = one
-    out[...] = turned[...].astype(jnp.bfloat16).reshape(out.shape)
+    out[...] = turned[: columns * snaps].astype(jnp.bfloat16).reshape(out.shape)
 
 
 def spectra_of(samples, bins, part, parts):
@@ -87,8 +87,8 @@
         out_specs=pl.BlockSpec(memory_space=pltpu.VMEM),
         scratch_shapes=[
             pltpu.VMEM((sensors, snaps, ticks), jnp.bfloat16),
-            pltpu.VMEM((sensors * snaps, 128), jnp.float32),
-            pltpu.VMEM((columns * snaps, sensors), jnp.float32),
+            pltpu.VMEM(((sensors + 1) * snaps, 128), jnp.float32),
+            pltpu.VMEM(((columns + 1) * snaps, sensors), jnp.float32),
             pltpu.SMEM(bins.shape, bins.dtype),
             pltpu.SemaphoreType.DMA((steps,)),
             pltpu.SemaphoreType.DMA(()),

time: 82.4 us -> 82.4 us (level)
  no operation moved by 1% of the time
where the time goes in v6:
time: 82.4 us; the launch traced here: 82.2 us
  blocking collectives  31.2 us (38%)
  waiting for transfers between devices  24.3 us (29%)
  starting transfers between devices  15.4 us (19%)
  Pallas kernels  10.9 us (13%)
    ppermute x8, waiting for transfers between devices, pass_on(): return [lax.ppermute(x, 'q', pairs) for x in pieces]  21.7 us
    all_to_all x1, blocking collectives, local(): mine = lax.all_to_all(mine, ('y', 'x'), 0, 0)  17.3 us
    all_to_all x1, blocking collectives, local(): mine = lax.all_to_all(mine, ('q', 'zh'), 0, 0)  14 us
    ppermute x8, starting transfers between devices, pass_on(): return [lax.ppermute(x, 'q', pairs) for x in pieces]  9.67 us
    pallas_call x2, Pallas kernels, spectra_of(): pl.pallas_call(functools.partial(spectra_kernel, part, steps), out_shape=...  6.76 us
    ppermute x1, starting transfers between devices, local(): other = lax.ppermute(mine, 'core', SWAP)  3.29 us
    ppermute x1, starting transfers between devices, local(): theirs = lax.ppermute(send, 'core', SWAP)  2.44 us
    pallas_call x1, Pallas kernels, load(): pl.pallas_call(load_kernel, out_shape=jax.ShapeDtypeStruct((chans, sensor...  2.21 us
  transfers between devices with their start and end apart: 10, of which 6 were waited for; matrix products, arithmetic and copies ran while one was open for 0% of the time, Pallas kernels for 7%

profile of v6, /device:TPU:1, one launch (start us, length us, event | category | flops | bytes accessed | tf_op | source)
XLA Modules:
  0.0 82.2 jit_solution(14598363456428705895)
XLA Ops:
  0.0 3.4 %spectra.2 = bf16[64,16,128]{2,1,0:T(8,128)(2,1)S(1)} custom-call(s32[32]{0:T(128)} %bins_in.3, bf16[256,16,1024]{2,1,0:T(8,128)(2,1)} %samples.3), custom_call_target="tpu_custom_call" | custom-call | flops 268435456 | bytes 4456448 | tf_op jit(solution)/shard_map/spectra/pallas_call | solution.py:83
  3.4 3.9 %collective-permute-start.2 = (bf16[2,32,16,128]{3,2,1,0:T(8,128)(2,1)S(1)}, bf16[2,32,16,128]{3,2,1,0:T(8,128)(2,1)S(1)}, u32[]{:S(2)}, u32[]{:S(2)}) collective-permute-start(bf16[2,32,16,128]{3,2,1,0:T(8,128)(2,1)S(1)} %bitcast.4), channel_id=1, source_target_pairs={{0,2},{2,0},{1,3},{3,1},{4,6},{6,4},{5,7},{7,5},{8,10},{10,8},{9,1... | collective-permute-start | bytes 786440 | tf_op jit(solution)/shard_map/ppermute | solution.py:251
  7.3 1.6 %collective-permute-start = (bf16[2,32,16,128]{3,2,1,0:T(8,128)(2,1)S(1)}, bf16[2,32,16,128]{3,2,1,0:T(8,128)(2,1)S(1)}, u32[]{:S(2)}, u32[]{:S(2)}) collective-permute-start(bf16[2,32,16,128]{3,2,1,0:T(8,128)(2,1)S(1)} %bitcast.5), channel_id=1, source_target_pairs={{0,1},{1,0},{2,3},{3,2},{4,5},{5,4},{6,7},{7,6},{8,9},{9,8},{10,11... | collective-permute-start | bytes 786440 | tf_op jit(solution)/shard_map/ppermute | solution.py:251
  8.9 3.4 %spectra.3 = bf16[64,16,128]{2,1,0:T(8,128)(2,1)S(1)} custom-call(s32[32]{0:T(128)} %bins_in.3, bf16[256,16,1024]{2,1,0:T(8,128)(2,1)} %samples.3), custom_call_target="tpu_custom_call" | custom-call | flops 268435456 | bytes 4456448 | tf_op jit(solution)/shard_map/spectra/pallas_call | solution.py:83
  12.3 0.2 collective-permute-start.3
  12.5 0.0 collective-permute-start.1
  12.5 5.8 %collective-permute-done.2.refs_4_ = bf16[2,32,16,128]{3,2,1,0:T(8,128)(2,1)S(1)} collective-permute-done((bf16[2,32,16,128]{3,2,1,0:T(8,128)(2,1)S(1)}, bf16[2,32,16,128]{3,2,1,0:T(8,128)(2,1)S(1)}, u32[]{:S(2)}, u32[]{:S(2)}) %collective-permute-start.2) | collective-permute-done | bytes 262176 | tf_op jit(solution)/shard_map/ppermute | solution.py:251
  18.3 0.7 collective-permute-start.4
  19.0 0.7 collective-permute-start.5
  19.7 0.0 collective-permute-done.refs_2_
  19.7 1.3 %collective-permute-start.6 = (bf16[2,32,16,128]{3,2,1,0:T(8,128)(2,1)S(1)}, bf16[2,32,16,128]{3,2,1,0:T(8,128)(2,1)S(1)}, u32[]{:S(2)}, u32[]{:S(2)}) collective-permute-start(bf16[2,32,16,128]{3,2,1,0:T(8,128)(2,1)S(1)} %collective-permute-done.2.refs_4_), channel_id=1, source_target_pairs={{2,3},{1,0},{6,7},{5,4},{10,11},{9,8},{14,15},{13,12},{18,19},{17,... | collective-permute-start | bytes 786440 | tf_op jit(solution)/shard_map/ppermute | solution.py:251
  21.0 8.6 %collective-permute-done.3.refs_5_ = bf16[2,32,16,128]{3,2,1,0:T(8,128)(2,1)S(1)} collective-permute-done((bf16[2,32,16,128]{3,2,1,0:T(8,128)(2,1)S(1)}, bf16[2,32,16,128]{3,2,1,0:T(8,128)(2,1)S(1)}, u32[]{:S(2)}, u32[]{:S(2)}) %collective-permute-start.3) | collective-permute-done | bytes 262176 | tf_op jit(solution)/shard_map/ppermute | solution.py:251
  29.6 1.3 %collective-permute-start.7 = (bf16[2,32,16,128]{3,2,1,0:T(8,128)(2,1)S(1)}, bf16[2,32,16,128]{3,2,1,0:T(8,128)(2,1)S(1)}, u32[]{:S(2)}, u32[]{:S(2)}) collective-permute-start(bf16[2,32,16,128]{3,2,1,0:T(8,128)(2,1)S(1)} %collective-permute-done.3.refs_5_), channel_id=1, source_target_pairs={{2,3},{1,0},{6,7},{5,4},{10,11},{9,8},{14,15},{13,12},{18,19},{17,... | collective-permute-start | bytes 786440 | tf_op jit(solution)/shard_map/ppermute | solution.py:251
  30.9 2.2 %load.1.refs_10_ = bf16[32,256,256]{2,1,0:T(8,128)(2,1)S(1)} custom-call(bf16[2,32,256,128]{3,2,1,0:T(8,128)(2,1)} %weights), custom_call_target="tpu_custom_call" | custom-call | bytes 8388608 | tf_op jit(solution)/shard_map/load/pallas_call | solution.py:126
  33.1 0.0 collective-permute-done.1.refs_3_
  33.1 0.0 collective-permute-done.4.refs_6_
  33.1 0.0 collective-permute-done.5.refs_7_
  33.1 1.7 %collective-permute-done.6.refs_8_ = bf16[2,32,16,128]{3,2,1,0:T(8,128)(2,1)S(1)} collective-permute-done((bf16[2,32,16,128]{3,2,1,0:T(8,128)(2,1)S(1)}, bf16[2,32,16,128]{3,2,1,0:T(8,128)(2,1)S(1)}, u32[]{:S(2)}, u32[]{:S(2)}) %collective-permute-start.6) | collective-permute-done | bytes 262176 | tf_op jit(solution)/shard_map/ppermute | solution.py:251
  34.9 5.6 %collective-permute-done.7.refs_9_ = bf16[2,32,16,128]{3,2,1,0:T(8,128)(2,1)S(1)} collective-permute-done((bf16[2,32,16,128]{3,2,1,0:T(8,128)(2,1)S(1)}, bf16[2,32,16,128]{3,2,1,0:T(8,128)(2,1)S(1)}, u32[]{:S(2)}, u32[]{:S(2)}) %collective-permute-start.7) | collective-permute-done | bytes 262176 | tf_op jit(solution)/shard_map/ppermute | solution.py:251
  40.5 0.8 beams.1
  41.3 2.4 %collective-permute-start.8 = (bf16[16,2,64,128]{3,2,1,0:T(8,128)(2,1)S(1)}, bf16[16,2,64,128]{3,2,1,0:T(8,128)(2,1)S(1)}, u32[]{:S(2)}, u32[]{:S(2)}) collective-permute-start(bf16[16,2,64,128]{3,2,1,0:T(8,128)(2,1)S(1)} %get-tuple-element.14), channel_id=1, source_target_pairs={{0,4},{4,0},{1,5},{5,1},{2,6},{6,2},{3,7},{7,3},{8,12},{12,8},{9,1... | collective-permute-start | bytes 1572872 | tf_op jit(solution)/shard_map/ppermute | solution.py:263
  43.7 1.5 %collective-permute-done.8 = bf16[16,2,64,128]{3,2,1,0:T(8,128)(2,1)S(1)} collective-permute-done((bf16[16,2,64,128]{3,2,1,0:T(8,128)(2,1)S(1)}, bf16[16,2,64,128]{3,2,1,0:T(8,128)(2,1)S(1)}, u32[]{:S(2)}, u32[]{:S(2)}) %collective-permute-start.8) | collective-permute-done | bytes 524320 | tf_op jit(solution)/shard_map/ppermute | solution.py:263
  45.3 0.1 add_convert_fusion
  45.4 17.3 %all_to_all.10 = bf16[16,2,64,128]{3,2,1,0:T(8,128)(2,1)S(1)} all-to-all(bf16[16,2,64,128]{3,2,1,0:T(8,128)(2,1)S(1)} %add_convert_fusion), channel_id=1, replica_groups=mesh['y'=4,'zh'=2,'x'=4,'core'=2,'q'=4] {'y','x'}, dimensions={0} | all-to-all | bytes 1048576 | tf_op jit(solution)/shard_map/all_to_all | solution.py:265
  62.7 0.1 reduce_sum.12
  62.8 14.0 %all_to_all.11 = bf16[8,64,128]{2,1,0:T(8,128)(2,1)S(1)} all-to-all(bf16[8,64,128]{2,1,0:T(8,128)(2,1)S(1)} %bitcast.14), channel_id=1, replica_groups=mesh['y'=4,'zh'=2,'x'=4,'core'=2,'q'=4] {'q','zh'}, dimensions={0} | all-to-all | bytes 262144 | tf_op jit(solution)/shard_map/all_to_all | solution.py:269
  76.8 3.3 %collective-permute-start.9 = (bf16[4,2,64,128]{3,2,1,0:T(8,128)(2,1)S(1)}, bf16[4,2,64,128]{3,2,1,0:T(8,128)(2,1)S(1)}, u32[]{:S(2)}, u32[]{:S(2)}) collective-permute-start(bf16[4,2,64,128]{3,2,1,0:T(8,128)(2,1)S(1)} %bitcast.12), channel_id=1, source_target_pairs={{0,4},{4,0},{1,5},{5,1},{2,6},{6,2},{3,7},{7,3},{8,12},{12,8},{9,1... | collective-permute-start | bytes 393224 | tf_op jit(solution)/shard_map/ppermute | solution.py:271
  80.0 1.0 %collective-permute-done.9.other = bf16[4,2,64,128]{3,2,1,0:T(8,128)(2,1)S(1)} collective-permute-done((bf16[4,2,64,128]{3,2,1,0:T(8,128)(2,1)S(1)}, bf16[4,2,64,128]{3,2,1,0:T(8,128)(2,1)S(1)}, u32[]{:S(2)}, u32[]{:S(2)}) %collective-permute-start.9) | collective-permute-done | bytes 131104 | tf_op jit(solution)/shard_map/ppermute | solution.py:271
  81.0 1.2 %gram.1 = f32[2,1,128,256]{3,2,1,0:T(8,128)} custom-call(bf16[4,2,64,128]{3,2,1,0:T(8,128)(2,1)S(1)} %bitcast.13, bf16[4,2,64,128]{3,2,1,0:T(8,128)(2,1)S(1)} %collective-permute-done.9.other), custom_call_target="tpu_custom_call" | custom-call | tf_op jit(solution)/shard_map/gram/pallas_call | solution.py:233
  (1 shorter events, 0.0 us)
Async XLA Ops:
  3.4 14.9 %collective-permute-start.2 = (bf16[2,32,16,128]{3,2,1,0:T(8,128)(2,1)S(1)}, bf16[2,32,16,128]{3,2,1,0:T(8,128)(2,1)S(1)}, u32[]{:S(2)}, u32[]{:S(2)}) collective-permute-start(bf16[2,32,16,128]{3,2,1,0:T(8,128)(2,1)S(1)} %bitcast.4), channel_id=1, source_target_pairs={{0,2},{2,0},{1,3},{3,1},{4,6},{6,4},{5,7},{7,5},{8,10},{10,8},{9,1... | collective-permute-start | bytes 786440 | tf_op jit(solution)/shard_map/ppermute | solution.py:251
  7.3 12.4 %collective-permute-start = (bf16[2,32,16,128]{3,2,1,0:T(8,128)(2,1)S(1)}, bf16[2,32,16,128]{3,2,1,0:T(8,128)(2,1)S(1)}, u32[]{:S(2)}, u32[]{:S(2)}) collective-permute-start(bf16[2,32,16,128]{3,2,1,0:T(8,128)(2,1)S(1)} %bitcast.5), channel_id=1, source_target_pairs={{0,1},{1,0},{2,3},{3,2},{4,5},{5,4},{6,7},{7,6},{8,9},{9,8},{10,11... | collective-permute-start | bytes 786440 | tf_op jit(solution)/shard_map/ppermute | solution.py:251
  12.3 17.2 %collective-permute-start.3 = (bf16[2,32,16,128]{3,2,1,0:T(8,128)(2,1)S(1)}, bf16[2,32,16,128]{3,2,1,0:T(8,128)(2,1)S(1)}, u32[]{:S(2)}, u32[]{:S(2)}) collective-permute-start(bf16[2,32,16,128]{3,2,1,0:T(8,128)(2,1)S(1)} %bitcast.8), channel_id=1, source_target_pairs={{0,2},{2,0},{1,3},{3,1},{4,6},{6,4},{5,7},{7,5},{8,10},{10,8},{9,1... | collective-permute-start | bytes 786440 | tf_op jit(solution)/shard_map/ppermute | solution.py:251
  12.5 20.6 %collective-permute-start.1 = (bf16[2,32,16,128]{3,2,1,0:T(8,128)(2,1)S(1)}, bf16[2,32,16,128]{3,2,1,0:T(8,128)(2,1)S(1)}, u32[]{:S(2)}, u32[]{:S(2)}) collective-permute-start(bf16[2,32,16,128]{3,2,1,0:T(8,128)(2,1)S(1)} %bitcast.9), channel_id=1, source_target_pairs={{0,1},{1,0},{2,3},{3,2},{4,5},{5,4},{6,7},{7,6},{8,9},{9,8},{10,11... | collective-permute-start | bytes 786440 | tf_op jit(solution)/shard_map/ppermute | solution.py:251
  18.3 14.8 %collective-permute-start.4 = (bf16[2,32,16,128]{3,2,1,0:T(8,128)(2,1)S(1)}, bf16[2,32,16,128]{3,2,1,0:T(8,128)(2,1)S(1)}, u32[]{:S(2)}, u32[]{:S(2)}) collective-permute-start(bf16[2,32,16,128]{3,2,1,0:T(8,128)(2,1)S(1)} %bitcast.6), channel_id=1, source_target_pairs={{1,2},{2,1},{5,6},{6,5},{9,10},{10,9},{13,14},{14,13},{17,18},{18,... | collective-permute-start | bytes 786440 | tf_op jit(solution)/shard_map/ppermute | solution.py:251
  19.0 14.1 %collective-permute-start.5 = (bf16[2,32,16,128]{3,2,1,0:T(8,128)(2,1)S(1)}, bf16[2,32,16,128]{3,2,1,0:T(8,128)(2,1)S(1)}, u32[]{:S(2)}, u32[]{:S(2)}) collective-permute-start(bf16[2,32,16,128]{3,2,1,0:T(8,128)(2,1)S(1)} %bitcast.10), channel_id=1, source_target_pairs={{1,2},{2,1},{5,6},{6,5},{9,10},{10,9},{13,14},{14,13},{17,18},{18,... | collective-permute-start | bytes 786440 | tf_op jit(solution)/shard_map/ppermute | solution.py:251
  19.7 15.2 %collective-permute-start.6 = (bf16[2,32,16,128]{3,2,1,0:T(8,128)(2,1)S(1)}, bf16[2,32,16,128]{3,2,1,0:T(8,128)(2,1)S(1)}, u32[]{:S(2)}, u32[]{:S(2)}) collective-permute-start(bf16[2,32,16,128]{3,2,1,0:T(8,128)(2,1)S(1)} %collective-permute-done.2.refs_4_), channel_id=1, source_target_pairs={{2,3},{1,0},{6,7},{5,4},{10,11},{9,8},{14,15},{13,12},{18,19},{17,... | collective-permute-start | bytes 786440 | tf_op jit(solution)/shard_map/ppermute | solution.py:251
  29.6 10.9 %collective-permute-start.7 = (bf16[2,32,16,128]{3,2,1,0:T(8,128)(2,1)S(1)}, bf16[2,32,16,128]{3,2,1,0:T(8,128)(2,1)S(1)}, u32[]{:S(2)}, u32[]{:S(2)}) collective-permute-start(bf16[2,32,16,128]{3,2,1,0:T(8,128)(2,1)S(1)} %collective-permute-done.3.refs_5_), channel_id=1, source_target_pairs={{2,3},{1,0},{6,7},{5,4},{10,11},{9,8},{14,15},{13,12},{18,19},{17,... | collective-permute-start | bytes 786440 | tf_op jit(solution)/shard_map/ppermute | solution.py:251
  41.3 4.0 %collective-permute-start.8 = (bf16[16,2,64,128]{3,2,1,0:T(8,128)(2,1)S(1)}, bf16[16,2,64,128]{3,2,1,0:T(8,128)(2,1)S(1)}, u32[]{:S(2)}, u32[]{:S(2)}) collective-permute-start(bf16[16,2,64,128]{3,2,1,0:T(8,128)(2,1)S(1)} %get-tuple-element.14), channel_id=1, source_target_pairs={{0,4},{4,0},{1,5},{5,1},{2,6},{6,2},{3,7},{7,3},{8,12},{12,8},{9,1... | collective-permute-start | bytes 1572872 | tf_op jit(solution)/shard_map/ppermute | solution.py:263
  76.8 4.3 %collective-permute-start.9 = (bf16[4,2,64,128]{3,2,1,0:T(8,128)(2,1)S(1)}, bf16[4,2,64,128]{3,2,1,0:T(8,128)(2,1)S(1)}, u32[]{:S(2)}, u32[]{:S(2)}) collective-permute-start(bf16[4,2,64,128]{3,2,1,0:T(8,128)(2,1)S(1)} %bitcast.12), channel_id=1, source_target_pairs={{0,4},{4,0},{1,5},{5,1},{2,6},{6,2},{3,7},{7,3},{8,12},{12,8},{9,1... | collective-permute-start | bytes 393224 | tf_op jit(solution)/shard_map/ppermute | solution.py:271

commit v7 on v6

--- a/solution.py
+++ b/solution.py
@@ -215,12 +215,19 @@
     right = jnp.concatenate([columns(real_y), columns(imag_y)], axis=0)
     inverse = 1.0 / snaps
 
+    def halves(a):
+        high = a.astype(jnp.bfloat16)
+        return high, (a - high.astype(jnp.float32)).astype(jnp.bfloat16)
+
+    right_high, right_low = halves(right)
+    rights = jnp.concatenate([right_high, right_low, right_high], axis=0)
+
     def contract(left):
+        high, low = halves(left)
         return lax.dot_general(
-            left,
-            right,
+            jnp.concatenate([high, high, low], axis=0),
+            rights,
             (((0,), (0,)), ((), ())),
-            precision=lax.Precision.HIGHEST,
             preferred_element_type=jnp.float32,
         )
 

time: 82.4 us -> 82.3 us (level)
  no operation moved by 1% of the time
where the time goes in v7:
time: 82.3 us; the launch traced here: 82 us
  blocking collectives  31.2 us (38%)
  waiting for transfers between devices  24.3 us (30%)
  starting transfers between devices  15.4 us (19%)
  Pallas kernels  10.8 us (13%)
    ppermute x8, waiting for transfers between devices, pass_on(): return [lax.ppermute(x, 'q', pairs) for x in pieces]  21.7 us
    all_to_all x1, blocking collectives, local(): mine = lax.all_to_all(mine, ('y', 'x'), 0, 0)  17.3 us
    all_to_all x1, blocking collectives, local(): mine = lax.all_to_all(mine, ('q', 'zh'), 0, 0)  14 us
    ppermute x8, starting transfers between devices, pass_on(): return [lax.ppermute(x, 'q', pairs) for x in pieces]  9.67 us
    pallas_call x2, Pallas kernels, spectra_of(): pl.pallas_call(functools.partial(spectra_kernel, part, steps), out_shape=...  6.76 us
    ppermute x1, starting transfers between devices, local(): other = lax.ppermute(mine, 'core', SWAP)  3.29 us
    ppermute x1, starting transfers between devices, local(): theirs = lax.ppermute(send, 'core', SWAP)  2.44 us
    pallas_call x1, Pallas kernels, load(): pl.pallas_call(load_kernel, out_shape=jax.ShapeDtypeStruct((chans, sensor...  2.21 us
  transfers between devices with their start and end apart: 10, of which 6 were waited for; matrix products, arithmetic and copies ran while one was open for 0% of the time, Pallas kernels for 7%

profile of v7, /device:TPU:1, one launch (start us, length us, event | category | flops | bytes accessed | tf_op | source)
XLA Modules:
  0.0 82.0 jit_solution(4985159955685204603)
XLA Ops:
  0.0 3.4 %spectra.2 = bf16[64,16,128]{2,1,0:T(8,128)(2,1)S(1)} custom-call(s32[32]{0:T(128)} %bins_in.3, bf16[256,16,1024]{2,1,0:T(8,128)(2,1)} %samples.3), custom_call_target="tpu_custom_call" | custom-call | flops 268435456 | bytes 4456448 | tf_op jit(solution)/shard_map/spectra/pallas_call | solution.py:83
  3.4 3.9 %collective-permute-start.2 = (bf16[2,32,16,128]{3,2,1,0:T(8,128)(2,1)S(1)}, bf16[2,32,16,128]{3,2,1,0:T(8,128)(2,1)S(1)}, u32[]{:S(2)}, u32[]{:S(2)}) collective-permute-start(bf16[2,32,16,128]{3,2,1,0:T(8,128)(2,1)S(1)} %bitcast.4), channel_id=1, source_target_pairs={{0,2},{2,0},{1,3},{3,1},{4,6},{6,4},{5,7},{7,5},{8,10},{10,8},{9,1... | collective-permute-start | bytes 786440 | tf_op jit(solution)/shard_map/ppermute | solution.py:258
  7.3 1.6 %collective-permute-start = (bf16[2,32,16,128]{3,2,1,0:T(8,128)(2,1)S(1)}, bf16[2,32,16,128]{3,2,1,0:T(8,128)(2,1)S(1)}, u32[]{:S(2)}, u32[]{:S(2)}) collective-permute-start(bf16[2,32,16,128]{3,2,1,0:T(8,128)(2,1)S(1)} %bitcast.5), channel_id=1, source_target_pairs={{0,1},{1,0},{2,3},{3,2},{4,5},{5,4},{6,7},{7,6},{8,9},{9,8},{10,11... | collective-permute-start | bytes 786440 | tf_op jit(solution)/shard_map/ppermute | solution.py:258
  8.9 3.4 %spectra.3 = bf16[64,16,128]{2,1,0:T(8,128)(2,1)S(1)} custom-call(s32[32]{0:T(128)} %bins_in.3, bf16[256,16,1024]{2,1,0:T(8,128)(2,1)} %samples.3), custom_call_target="tpu_custom_call" | custom-call | flops 268435456 | bytes 4456448 | tf_op jit(solution)/shard_map/spectra/pallas_call | solution.py:83
  12.3 0.2 collective-permute-start.3
  12.5 0.0 collective-permute-start.1
  12.5 5.8 %collective-permute-done.2.refs_4_ = bf16[2,32,16,128]{3,2,1,0:T(8,128)(2,1)S(1)} collective-permute-done((bf16[2,32,16,128]{3,2,1,0:T(8,128)(2,1)S(1)}, bf16[2,32,16,128]{3,2,1,0:T(8,128)(2,1)S(1)}, u32[]{:S(2)}, u32[]{:S(2)}) %collective-permute-start.2) | collective-permute-done | bytes 262176 | tf_op jit(solution)/shard_map/ppermute | solution.py:258
  18.3 0.7 collective-permute-start.4
  19.0 0.7 collective-permute-start.5
  19.7 0.0 collective-permute-done.refs_2_
  19.7 1.3 %collective-permute-start.6 = (bf16[2,32,16,128]{3,2,1,0:T(8,128)(2,1)S(1)}, bf16[2,32,16,128]{3,2,1,0:T(8,128)(2,1)S(1)}, u32[]{:S(2)}, u32[]{:S(2)}) collective-permute-start(bf16[2,32,16,128]{3,2,1,0:T(8,128)(2,1)S(1)} %collective-permute-done.2.refs_4_), channel_id=1, source_target_pairs={{2,3},{1,0},{6,7},{5,4},{10,11},{9,8},{14,15},{13,12},{18,19},{17,... | collective-permute-start | bytes 786440 | tf_op jit(solution)/shard_map/ppermute | solution.py:258
  21.0 8.6 %collective-permute-done.3.refs_5_ = bf16[2,32,16,128]{3,2,1,0:T(8,128)(2,1)S(1)} collective-permute-done((bf16[2,32,16,128]{3,2,1,0:T(8,128)(2,1)S(1)}, bf16[2,32,16,128]{3,2,1,0:T(8,128)(2,1)S(1)}, u32[]{:S(2)}, u32[]{:S(2)}) %collective-permute-start.3) | collective-permute-done | bytes 262176 | tf_op jit(solution)/shard_map/ppermute | solution.py:258
  29.6 1.3 %collective-permute-start.7 = (bf16[2,32,16,128]{3,2,1,0:T(8,128)(2,1)S(1)}, bf16[2,32,16,128]{3,2,1,0:T(8,128)(2,1)S(1)}, u32[]{:S(2)}, u32[]{:S(2)}) collective-permute-start(bf16[2,32,16,128]{3,2,1,0:T(8,128)(2,1)S(1)} %collective-permute-done.3.refs_5_), channel_id=1, source_target_pairs={{2,3},{1,0},{6,7},{5,4},{10,11},{9,8},{14,15},{13,12},{18,19},{17,... | collective-permute-start | bytes 786440 | tf_op jit(solution)/shard_map/ppermute | solution.py:258
  30.9 2.2 %load.1.refs_10_ = bf16[32,256,256]{2,1,0:T(8,128)(2,1)S(1)} custom-call(bf16[2,32,256,128]{3,2,1,0:T(8,128)(2,1)} %weights), custom_call_target="tpu_custom_call" | custom-call | bytes 8388608 | tf_op jit(solution)/shard_map/load/pallas_call | solution.py:126
  33.1 0.0 collective-permute-done.1.refs_3_
  33.1 0.0 collective-permute-done.4.refs_6_
  33.1 0.0 collective-permute-done.5.refs_7_
  33.1 1.7 %collective-permute-done.6.refs_8_ = bf16[2,32,16,128]{3,2,1,0:T(8,128)(2,1)S(1)} collective-permute-done((bf16[2,32,16,128]{3,2,1,0:T(8,128)(2,1)S(1)}, bf16[2,32,16,128]{3,2,1,0:T(8,128)(2,1)S(1)}, u32[]{:S(2)}, u32[]{:S(2)}) %collective-permute-start.6) | collective-permute-done | bytes 262176 | tf_op jit(solution)/shard_map/ppermute | solution.py:258
  34.9 5.6 %collective-permute-done.7.refs_9_ = bf16[2,32,16,128]{3,2,1,0:T(8,128)(2,1)S(1)} collective-permute-done((bf16[2,32,16,128]{3,2,1,0:T(8,128)(2,1)S(1)}, bf16[2,32,16,128]{3,2,1,0:T(8,128)(2,1)S(1)}, u32[]{:S(2)}, u32[]{:S(2)}) %collective-permute-start.7) | collective-permute-done | bytes 262176 | tf_op jit(solution)/shard_map/ppermute | solution.py:258
  40.5 0.8 beams.1
  41.3 2.4 %collective-permute-start.8 = (bf16[16,2,64,128]{3,2,1,0:T(8,128)(2,1)S(1)}, bf16[16,2,64,128]{3,2,1,0:T(8,128)(2,1)S(1)}, u32[]{:S(2)}, u32[]{:S(2)}) collective-permute-start(bf16[16,2,64,128]{3,2,1,0:T(8,128)(2,1)S(1)} %get-tuple-element.14), channel_id=1, source_target_pairs={{0,4},{4,0},{1,5},{5,1},{2,6},{6,2},{3,7},{7,3},{8,12},{12,8},{9,1... | collective-permute-start | bytes 1572872 | tf_op jit(solution)/shard_map/ppermute | solution.py:270
  43.7 1.5 %collective-permute-done.8 = bf16[16,2,64,128]{3,2,1,0:T(8,128)(2,1)S(1)} collective-permute-done((bf16[16,2,64,128]{3,2,1,0:T(8,128)(2,1)S(1)}, bf16[16,2,64,128]{3,2,1,0:T(8,128)(2,1)S(1)}, u32[]{:S(2)}, u32[]{:S(2)}) %collective-permute-start.8) | collective-permute-done | bytes 524320 | tf_op jit(solution)/shard_map/ppermute | solution.py:270
  45.3 0.1 add_convert_fusion
  45.4 17.3 %all_to_all.10 = bf16[16,2,64,128]{3,2,1,0:T(8,128)(2,1)S(1)} all-to-all(bf16[16,2,64,128]{3,2,1,0:T(8,128)(2,1)S(1)} %add_convert_fusion), channel_id=1, replica_groups=mesh['y'=4,'zh'=2,'x'=4,'core'=2,'q'=4] {'y','x'}, dimensions={0} | all-to-all | bytes 1048576 | tf_op jit(solution)/shard_map/all_to_all | solution.py:272
  62.7 0.1 reduce_sum.12
  62.8 14.0 %all_to_all.11 = bf16[8,64,128]{2,1,0:T(8,128)(2,1)S(1)} all-to-all(bf16[8,64,128]{2,1,0:T(8,128)(2,1)S(1)} %bitcast.14), channel_id=1, replica_groups=mesh['y'=4,'zh'=2,'x'=4,'core'=2,'q'=4] {'q','zh'}, dimensions={0} | all-to-all | bytes 262144 | tf_op jit(solution)/shard_map/all_to_all | solution.py:276
  76.8 3.3 %collective-permute-start.9 = (bf16[4,2,64,128]{3,2,1,0:T(8,128)(2,1)S(1)}, bf16[4,2,64,128]{3,2,1,0:T(8,128)(2,1)S(1)}, u32[]{:S(2)}, u32[]{:S(2)}) collective-permute-start(bf16[4,2,64,128]{3,2,1,0:T(8,128)(2,1)S(1)} %bitcast.12), channel_id=1, source_target_pairs={{0,4},{4,0},{1,5},{5,1},{2,6},{6,2},{3,7},{7,3},{8,12},{12,8},{9,1... | collective-permute-start | bytes 393224 | tf_op jit(solution)/shard_map/ppermute | solution.py:278
  80.0 1.0 %collective-permute-done.9.other = bf16[4,2,64,128]{3,2,1,0:T(8,128)(2,1)S(1)} collective-permute-done((bf16[4,2,64,128]{3,2,1,0:T(8,128)(2,1)S(1)}, bf16[4,2,64,128]{3,2,1,0:T(8,128)(2,1)S(1)}, u32[]{:S(2)}, u32[]{:S(2)}) %collective-permute-start.9) | collective-permute-done | bytes 131104 | tf_op jit(solution)/shard_map/ppermute | solution.py:278
  81.0 1.0 %gram.1 = f32[2,1,128,256]{3,2,1,0:T(8,128)} custom-call(bf16[4,2,64,128]{3,2,1,0:T(8,128)(2,1)S(1)} %bitcast.13, bf16[4,2,64,128]{3,2,1,0:T(8,128)(2,1)S(1)} %collective-permute-done.9.other), custom_call_target="tpu_custom_call" | custom-call | tf_op jit(solution)/shard_map/gram/pallas_call | solution.py:240
  (1 shorter events, 0.0 us)
Async XLA Ops:
  3.4 14.9 %collective-permute-start.2 = (bf16[2,32,16,128]{3,2,1,0:T(8,128)(2,1)S(1)}, bf16[2,32,16,128]{3,2,1,0:T(8,128)(2,1)S(1)}, u32[]{:S(2)}, u32[]{:S(2)}) collective-permute-start(bf16[2,32,16,128]{3,2,1,0:T(8,128)(2,1)S(1)} %bitcast.4), channel_id=1, source_target_pairs={{0,2},{2,0},{1,3},{3,1},{4,6},{6,4},{5,7},{7,5},{8,10},{10,8},{9,1... | collective-permute-start | bytes 786440 | tf_op jit(solution)/shard_map/ppermute | solution.py:258
  7.3 12.4 %collective-permute-start = (bf16[2,32,16,128]{3,2,1,0:T(8,128)(2,1)S(1)}, bf16[2,32,16,128]{3,2,1,0:T(8,128)(2,1)S(1)}, u32[]{:S(2)}, u32[]{:S(2)}) collective-permute-start(bf16[2,32,16,128]{3,2,1,0:T(8,128)(2,1)S(1)} %bitcast.5), channel_id=1, source_target_pairs={{0,1},{1,0},{2,3},{3,2},{4,5},{5,4},{6,7},{7,6},{8,9},{9,8},{10,11... | collective-permute-start | bytes 786440 | tf_op jit(solution)/shard_map/ppermute | solution.py:258
  12.3 17.2 %collective-permute-start.3 = (bf16[2,32,16,128]{3,2,1,0:T(8,128)(2,1)S(1)}, bf16[2,32,16,128]{3,2,1,0:T(8,128)(2,1)S(1)}, u32[]{:S(2)}, u32[]{:S(2)}) collective-permute-start(bf16[2,32,16,128]{3,2,1,0:T(8,128)(2,1)S(1)} %bitcast.8), channel_id=1, source_target_pairs={{0,2},{2,0},{1,3},{3,1},{4,6},{6,4},{5,7},{7,5},{8,10},{10,8},{9,1... | collective-permute-start | bytes 786440 | tf_op jit(solution)/shard_map/ppermute | solution.py:258
  12.5 20.6 %collective-permute-start.1 = (bf16[2,32,16,128]{3,2,1,0:T(8,128)(2,1)S(1)}, bf16[2,32,16,128]{3,2,1,0:T(8,128)(2,1)S(1)}, u32[]{:S(2)}, u32[]{:S(2)}) collective-permute-start(bf16[2,32,16,128]{3,2,1,0:T(8,128)(2,1)S(1)} %bitcast.9), channel_id=1, source_target_pairs={{0,1},{1,0},{2,3},{3,2},{4,5},{5,4},{6,7},{7,6},{8,9},{9,8},{10,11... | collective-permute-start | bytes 786440 | tf_op jit(solution)/shard_map/ppermute | solution.py:258
  18.3 14.8 %collective-permute-start.4 = (bf16[2,32,16,128]{3,2,1,0:T(8,128)(2,1)S(1)}, bf16[2,32,16,128]{3,2,1,0:T(8,128)(2,1)S(1)}, u32[]{:S(2)}, u32[]{:S(2)}) collective-permute-start(bf16[2,32,16,128]{3,2,1,0:T(8,128)(2,1)S(1)} %bitcast.6), channel_id=1, source_target_pairs={{1,2},{2,1},{5,6},{6,5},{9,10},{10,9},{13,14},{14,13},{17,18},{18,... | collective-permute-start | bytes 786440 | tf_op jit(solution)/shard_map/ppermute | solution.py:258
  19.0 14.1 %collective-permute-start.5 = (bf16[2,32,16,128]{3,2,1,0:T(8,128)(2,1)S(1)}, bf16[2,32,16,128]{3,2,1,0:T(8,128)(2,1)S(1)}, u32[]{:S(2)}, u32[]{:S(2)}) collective-permute-start(bf16[2,32,16,128]{3,2,1,0:T(8,128)(2,1)S(1)} %bitcast.10), channel_id=1, source_target_pairs={{1,2},{2,1},{5,6},{6,5},{9,10},{10,9},{13,14},{14,13},{17,18},{18,... | collective-permute-start | bytes 786440 | tf_op jit(solution)/shard_map/ppermute | solution.py:258
  19.7 15.2 %collective-permute-start.6 = (bf16[2,32,16,128]{3,2,1,0:T(8,128)(2,1)S(1)}, bf16[2,32,16,128]{3,2,1,0:T(8,128)(2,1)S(1)}, u32[]{:S(2)}, u32[]{:S(2)}) collective-permute-start(bf16[2,32,16,128]{3,2,1,0:T(8,128)(2,1)S(1)} %collective-permute-done.2.refs_4_), channel_id=1, source_target_pairs={{2,3},{1,0},{6,7},{5,4},{10,11},{9,8},{14,15},{13,12},{18,19},{17,... | collective-permute-start | bytes 786440 | tf_op jit(solution)/shard_map/ppermute | solution.py:258
  29.6 10.9 %collective-permute-start.7 = (bf16[2,32,16,128]{3,2,1,0:T(8,128)(2,1)S(1)}, bf16[2,32,16,128]{3,2,1,0:T(8,128)(2,1)S(1)}, u32[]{:S(2)}, u32[]{:S(2)}) collective-permute-start(bf16[2,32,16,128]{3,2,1,0:T(8,128)(2,1)S(1)} %collective-permute-done.3.refs_5_), channel_id=1, source_target_pairs={{2,3},{1,0},{6,7},{5,4},{10,11},{9,8},{14,15},{13,12},{18,19},{17,... | collective-permute-start | bytes 786440 | tf_op jit(solution)/shard_map/ppermute | solution.py:258
  41.3 4.0 %collective-permute-start.8 = (bf16[16,2,64,128]{3,2,1,0:T(8,128)(2,1)S(1)}, bf16[16,2,64,128]{3,2,1,0:T(8,128)(2,1)S(1)}, u32[]{:S(2)}, u32[]{:S(2)}) collective-permute-start(bf16[16,2,64,128]{3,2,1,0:T(8,128)(2,1)S(1)} %get-tuple-element.14), channel_id=1, source_target_pairs={{0,4},{4,0},{1,5},{5,1},{2,6},{6,2},{3,7},{7,3},{8,12},{12,8},{9,1... | collective-permute-start | bytes 1572872 | tf_op jit(solution)/shard_map/ppermute | solution.py:270
  76.8 4.3 %collective-permute-start.9 = (bf16[4,2,64,128]{3,2,1,0:T(8,128)(2,1)S(1)}, bf16[4,2,64,128]{3,2,1,0:T(8,128)(2,1)S(1)}, u32[]{:S(2)}, u32[]{:S(2)}) collective-permute-start(bf16[4,2,64,128]{3,2,1,0:T(8,128)(2,1)S(1)} %bitcast.12), channel_id=1, source_target_pairs={{0,4},{4,0},{1,5},{5,1},{2,6},{6,2},{3,7},{7,3},{8,12},{12,8},{9,1... | collective-permute-start | bytes 393224 | tf_op jit(solution)/shard_map/ppermute | solution.py:278
